TPU v7x, 512 devices: a whole 4x8x8 slice. The times are simulated.
512 devices in a mesh: blk: 64 (over z, y), mode: 8 (over x, core).
Axes of the slice: x: 4, y: 8, z: 8, core: 2. Of those that a mesh axis runs over, the one named last changes fastest.
Arguments:
- start_modes: float32 [64, 3, 256, 16, 128], P('mode', None, 'blk'), may hold values from -6 to 6
- materials: int32 [256, 16, 128], P('blk'), may hold values from 0 to 7
- stiffness_table: float32 [8], replicated, may hold values from 0.25 to 4
Outputs:
- basis: float32 [64, 3, 256, 16, 128], P('mode', None, 'blk')
- projected: float32 [64, 64], replicated
All inputs are finite; a program needn't handle non-finite values.
Results may differ from a plain program's by a relative error of at most 0.00007.
Values sent between devices are 32-bit elements; how exact they have to be, the bound alone decides.
A program may use at most 64 MiB of HBM per device.

v0:
```python
import jax
import jax.numpy as jnp
from jax import lax
from jax.sharding import PartitionSpec as P

CENTER = 64.0
HALF_WIDTH = 56.0
MASS_SHIFT = 0.5


def extended(shard, sides, width):
    for axis, dim in sides:
        peers, length = (lax.axis_size(axis), shard.shape[dim])
        up = [(i, (i + 1) % peers) for i in range(peers - 1)]
        down = [(j, i) for i, j in up]
        last = lax.slice_in_dim(shard, length - width, length, axis=dim)
        initial = lax.slice_in_dim(shard, 0, width, axis=dim)
        before = lax.ppermute(last, axis, up)
        after = lax.ppermute(initial, axis, down)
        shard = jnp.concatenate([before, shard, after], axis=dim)
    return shard


def stiffness_root(materials, stiffness_table):
    count = stiffness_table.shape[0]
    labels = jnp.arange(count, dtype=jnp.int32).reshape((count, 1, 1, 1))
    indicator = (materials[None] == labels).astype(jnp.float32)
    return jnp.sqrt(jnp.sum(indicator * stiffness_table.reshape((count, 1, 1, 1)), axis=0))


def operate(field, stiff_root):
    weighted = stiff_root * field
    padded = extended(weighted, (("blk", 2),), 1)
    along_x = padded[:, :, :-2] + padded[:, :, 1:-1] + padded[:, :, 2:]
    wide_y = jnp.pad(along_x, ((0, 0), (0, 0), (0, 0), (1, 1), (1, 1)))
    along_y = wide_y[:, :, :, :-2, :] + wide_y[:, :, :, 1:-1, :] + wide_y[:, :, :, 2:, :]
    boxed = along_y[..., :-2] + along_y[..., 1:-1] + along_y[..., 2:]
    return stiff_root * (27.0 * weighted - boxed) + MASS_SHIFT * field


def project_sums(filtered, image):
    modes = filtered.shape[0]
    flat_basis = filtered.reshape((modes, -1))
    flat_image = image.reshape((modes, -1))
    high = lax.Precision.HIGHEST
    gram_part = jnp.dot(flat_basis, flat_basis.T, precision=high)
    cross_part = jnp.dot(flat_basis, flat_image.T, precision=high)
    return (flat_basis, gram_part, cross_part)


def factorize(gram, cross):
    modes = gram.shape[0]
    high = lax.Precision.HIGHEST
    factor = jnp.linalg.cholesky(gram)
    identity = jnp.eye(modes, dtype=jnp.float32)
    inverse = lax.linalg.triangular_solve(factor, identity, left_side=True, lower=True)
    projected = jnp.dot(jnp.dot(inverse, cross, precision=high), inverse.T, precision=high)
    return (inverse, projected)


def shards(start_modes, materials, stiffness_table):
    stiff_root = stiffness_root(materials, stiffness_table)
    before = start_modes
    current = (operate(start_modes, stiff_root) - CENTER * start_modes) / HALF_WIDTH
    for degree_step in range(3):
        following = 2.0 * (operate(current, stiff_root) - CENTER * current) / HALF_WIDTH - before
        before, current = (current, following)
    image = operate(current, stiff_root)
    high = lax.Precision.HIGHEST
    gathered_basis, gathered_image = (
        lax.all_gather(current, "mode", axis=0, tiled=True),
        lax.all_gather(image, "mode", axis=0, tiled=True),
    )
    flat_basis, gram_part, cross_part = project_sums(gathered_basis, gathered_image)
    gram, cross = lax.psum((gram_part, cross_part), "blk")
    inverse, projected = factorize(gram, cross)
    local_modes = current.shape[0]
    own_rows = lax.dynamic_slice_in_dim(
        inverse, lax.axis_index("mode") * local_modes, local_modes, 0
    )
    basis = jnp.dot(own_rows, flat_basis, precision=high).reshape(current.shape)
    return (basis, projected)


def solution(mesh):
    return jax.shard_map(
        shards,
        mesh=mesh,
        in_specs=(P("mode", None, "blk", None, None), P("blk", None, None), P()),
        out_specs=(P("mode", None, "blk", None, None), P()),
        check_vma=False,
    )
```

profile of v0, /device:TPU:4, one launch (start us, length us, event | category | flops | bytes accessed | tf_op | source)
XLA Modules:
  0.0 495.5 jit_solution(1887299256201371727)
XLA Ops:
  8.1 1.6 copy_multiply_fusion
  9.7 3.5 collective-permute-start
  13.2 1.3 collective-permute-start.1
  14.5 2.8 collective-permute-done
  17.4 4.1 collective-permute-done.1
  23.6 3.5 collective-permute-start.2
  28.4 1.9 collective-permute-done.2
  30.2 5.1 %collective-permute-done.3 = f32[8,3,1,16,128]{4,0,3,2,1:T(8,128)S(1)} collective-permute-done((f32[8,3,1,16,128]{4,0,3,2,1:T(8,128)S(1)}, f32[8,3,1,16,128]{4,0,3,2,1:T(8,128)S(1)}, u32[]{:S(2)}, u32[]{:S(2)}) %collective-permute-start.3) | collective-permute-done | bytes 196640 | tf_op jit(solution)/shard_map/ppermute | solution.py:19
  37.5 4.8 collective-permute-start.4
  43.5 1.9 collective-permute-done.4
  45.4 4.4 collective-permute-done.5
  51.7 3.9 collective-permute-start.6
  55.6 1.3 collective-permute-start.7
  56.9 1.9 collective-permute-done.6
  58.8 4.4 collective-permute-done.7
  64.5 1.4 broadcast_multiply_fusion.1
  66.0 3.1 collective-permute-start.8
  69.1 1.5 collective-permute-start.9
  70.6 1.7 collective-permute-done.8
  72.3 4.4 collective-permute-done.9
  78.0 1.4 fusion.14
  79.4 43.2 %all-gather.3.cloned.1.call-done = f32[64,3,4,16,128]{4,0,3,2,1:T(8,128)} async-done(((f32[8,3,4,16,128]{4,0,3,2,1:T(8,128)}), f32[64,3,4,16,128]{4,0,3,2,1:T(8,128)}) %all-gather.3.cloned.1.call-update) | async-done | bytes 6291472 | tf_op jit(solution)/shard_map/all_gather | solution.py:71
  122.6 6.4 %copy.27 = f32[64,3,4,16,128]{4,3,2,1,0:T(8,128)S(1)} copy(f32[64,3,4,16,128]{4,0,3,2,1:T(8,128)} %all-gather.3.cloned.1.call-done) | data formatting | bytes 12582912 | tf_op jit(solution)/shard_map/all_gather | solution.py:71
  129.1 3.6 copy.46
  132.6 3.7 copy.35
  136.3 5.3 %convolution_bitcast_fusion.1 = f32[64,64]{0,1:T(8,128)S(1)} fusion(f32[64,3,4,16,128]{4,0,3,2,1:T(8,128)S(1)} %bitcast.42), kind=kOutput, calls=%fused_computation.29 | convolution fusion | flops 1207959552 | bytes 6307840 | tf_op jit(solution)/shard_map/dot_general | solution.py:46
  141.6 34.4 %all-gather.5.cloned.1.call-done = f32[64,3,4,16,128]{4,0,3,2,1:T(8,128)} async-done(((f32[8,3,4,16,128]{4,0,3,2,1:T(8,128)}), f32[64,3,4,16,128]{4,0,3,2,1:T(8,128)}) %all-gather.5.cloned.1.call-update) | async-done | bytes 6291472 | tf_op jit(solution)/shard_map/all_gather | solution.py:72
  176.1 8.2 %convolution_bitcast_fusion = f32[64,64]{1,0:T(8,128)S(1)} fusion(f32[64,3,4,16,128]{4,0,3,2,1:T(8,128)} %all-gather.3.cloned.1.call-done, f32[64,3,4,16,128]{4,0,3,2,1:T(8,128)} %all-gather.5.cloned.1.call-done), kind=kOutput, calls=%fused_computation.28 | convolution fusion | flops 1207959552 | bytes 12599296 | tf_op jit(solution)/shard_map/dot_general | solution.py:47
  184.2 280.4 %all-reduce.5 = (f32[64,64]{0,1:T(8,128)S(1)}, f32[64,64]{1,0:T(8,128)S(1)}) all-reduce(f32[64,64]{0,1:T(8,128)S(1)} %convolution_bitcast_fusion.1, f32[64,64]{1,0:T(8,128)S(1)} %convolution_bitcast_fusion), channel_id=1, replica_groups=mesh['blk'=64,'mode'=8] {'blk'}, use_global_device_ids=true, to_apply=%region_1.2 | all-reduce | flops 8192 | bytes 65536 | tf_op jit(solution)/shard_map/psum | solution.py:75
  464.8 5.8 %cholesky.17 = f32[64,64]{1,0:T(8,128)S(1)} custom-call(f32[64,64]{1,0:T(8,128)S(1)} %fusion.50), custom_call_target="Cholesky" | custom-call | tf_op jit(solution)/shard_map/jit(cholesky)/cholesky | solution.py:54
  472.0 4.9 custom-call.6
  478.1 9.6 %fusion = f32[8,3,4,16,128]{4,0,3,2,1:T(8,128)S(1)} fusion(f32[3,4,16,128,64]{3,2,1,0,4:T(8,128)} %bitcast.43, f32[64,64]{1,0:T(8,128)S(1)} %fusion.48, s32[]{:T(128)S(6)} %select_n.8), kind=kOutput, calls=%fused_computation.1 | convolution fusion | flops 150994944 | bytes 7081988 | tf_op jit(solution)/shard_map/dot_general | solution.py:81
  (44 shorter events, 15.9 us)
Async XLA Ops:
  7.2 115.4 %all-gather.3.cloned.1.call-start = ((), (), s32[]{:S(2)}) async-start(), calls=%async_computation | async-start | bytes 7077888 | tf_op jit(solution)/shard_map/all_gather | solution.py:71
  9.7 7.6 %collective-permute-start = (f32[8,3,1,16,128]{4,0,3,2,1:T(8,128)S(1)}, f32[8,3,1,16,128]{4,0,3,2,1:T(8,128)S(1)}, u32[]{:S(2)}, u32[]{:S(2)}) collective-permute-start(f32[8,3,1,16,128]{4,0,3,2,1:T(8,128)S(1)} %get-tuple-element.26), channel_id=1, source_target_pairs={{0,8},{8,16},{16,24},{24,32},{32,40},{40,48},{48,56},{56,64},{64,7... | collective-permute-start | bytes 589832 | tf_op jit(solution)/shard_map/ppermute | solution.py:18
  13.2 8.3 %collective-permute-start.1 = (f32[8,3,1,16,128]{4,0,3,2,1:T(8,128)S(1)}, f32[8,3,1,16,128]{4,0,3,2,1:T(8,128)S(1)}, u32[]{:S(2)}, u32[]{:S(2)}) collective-permute-start(f32[8,3,1,16,128]{4,0,3,2,1:T(8,128)S(1)} %get-tuple-element.27), channel_id=1, source_target_pairs={{8,0},{16,8},{24,16},{32,24},{40,32},{48,40},{56,48},{64,56},{72,6... | collective-permute-start | bytes 589832 | tf_op jit(solution)/shard_map/ppermute | solution.py:19
  21.6 1.2 copy-start
  23.6 6.7 %collective-permute-start.2 = (f32[8,3,1,16,128]{4,0,3,2,1:T(8,128)S(1)}, f32[8,3,1,16,128]{4,0,3,2,1:T(8,128)S(1)}, u32[]{:S(2)}, u32[]{:S(2)}) collective-permute-start(f32[8,3,1,16,128]{4,0,3,2,1:T(8,128)S(1)} %get-tuple-element.24), channel_id=1, source_target_pairs={{0,8},{8,16},{16,24},{24,32},{32,40},{40,48},{48,56},{56,64},{64,7... | collective-permute-start | bytes 589832 | tf_op jit(solution)/shard_map/ppermute | solution.py:18
  27.1 8.3 %collective-permute-start.3 = (f32[8,3,1,16,128]{4,0,3,2,1:T(8,128)S(1)}, f32[8,3,1,16,128]{4,0,3,2,1:T(8,128)S(1)}, u32[]{:S(2)}, u32[]{:S(2)}) collective-permute-start(f32[8,3,1,16,128]{4,0,3,2,1:T(8,128)S(1)} %get-tuple-element.25), channel_id=1, source_target_pairs={{8,0},{16,8},{24,16},{32,24},{40,32},{48,40},{56,48},{64,56},{72,6... | collective-permute-start | bytes 589832 | tf_op jit(solution)/shard_map/ppermute | solution.py:19
  37.5 7.9 %collective-permute-start.4 = (f32[8,3,1,16,128]{4,0,3,2,1:T(8,128)S(1)}, f32[8,3,1,16,128]{4,0,3,2,1:T(8,128)S(1)}, u32[]{:S(2)}, u32[]{:S(2)}) collective-permute-start(f32[8,3,1,16,128]{4,0,3,2,1:T(8,128)S(1)} %get-tuple-element.22), channel_id=1, source_target_pairs={{0,8},{8,16},{16,24},{24,32},{32,40},{40,48},{48,56},{56,64},{64,7... | collective-permute-start | bytes 589832 | tf_op jit(solution)/shard_map/ppermute | solution.py:18
  42.2 7.6 %collective-permute-start.5 = (f32[8,3,1,16,128]{4,0,3,2,1:T(8,128)S(1)}, f32[8,3,1,16,128]{4,0,3,2,1:T(8,128)S(1)}, u32[]{:S(2)}, u32[]{:S(2)}) collective-permute-start(f32[8,3,1,16,128]{4,0,3,2,1:T(8,128)S(1)} %get-tuple-element.23), channel_id=1, source_target_pairs={{8,0},{16,8},{24,16},{32,24},{40,32},{48,40},{56,48},{64,56},{72,6... | collective-permute-start | bytes 589832 | tf_op jit(solution)/shard_map/ppermute | solution.py:19
  51.7 7.1 %collective-permute-start.6 = (f32[8,3,1,16,128]{4,0,3,2,1:T(8,128)S(1)}, f32[8,3,1,16,128]{4,0,3,2,1:T(8,128)S(1)}, u32[]{:S(2)}, u32[]{:S(2)}) collective-permute-start(f32[8,3,1,16,128]{4,0,3,2,1:T(8,128)S(1)} %get-tuple-element.20), channel_id=1, source_target_pairs={{0,8},{8,16},{16,24},{24,32},{32,40},{40,48},{48,56},{56,64},{64,7... | collective-permute-start | bytes 589832 | tf_op jit(solution)/shard_map/ppermute | solution.py:18
  55.6 7.6 %collective-permute-start.7 = (f32[8,3,1,16,128]{4,0,3,2,1:T(8,128)S(1)}, f32[8,3,1,16,128]{4,0,3,2,1:T(8,128)S(1)}, u32[]{:S(2)}, u32[]{:S(2)}) collective-permute-start(f32[8,3,1,16,128]{4,0,3,2,1:T(8,128)S(1)} %get-tuple-element.21), channel_id=1, source_target_pairs={{8,0},{16,8},{24,16},{32,24},{40,32},{48,40},{56,48},{64,56},{72,6... | collective-permute-start | bytes 589832 | tf_op jit(solution)/shard_map/ppermute | solution.py:19
  65.9 110.2 %all-gather.5.cloned.1.call-start = ((), (), s32[]{:S(2)}) async-start(), calls=%async_computation.1 | async-start | bytes 7077888 | tf_op jit(solution)/shard_map/all_gather | solution.py:72
  66.0 6.3 %collective-permute-start.8 = (f32[8,3,1,16,128]{4,0,3,2,1:T(8,128)S(1)}, f32[8,3,1,16,128]{4,0,3,2,1:T(8,128)S(1)}, u32[]{:S(2)}, u32[]{:S(2)}) collective-permute-start(f32[8,3,1,16,128]{4,0,3,2,1:T(8,128)S(1)} %get-tuple-element.18), channel_id=1, source_target_pairs={{0,8},{8,16},{16,24},{24,32},{32,40},{40,48},{48,56},{56,64},{64,7... | collective-permute-start | bytes 589832 | tf_op jit(solution)/shard_map/ppermute | solution.py:18
  69.1 7.6 %collective-permute-start.9 = (f32[8,3,1,16,128]{4,0,3,2,1:T(8,128)S(1)}, f32[8,3,1,16,128]{4,0,3,2,1:T(8,128)S(1)}, u32[]{:S(2)}, u32[]{:S(2)}) collective-permute-start(f32[8,3,1,16,128]{4,0,3,2,1:T(8,128)S(1)} %get-tuple-element.19), channel_id=1, source_target_pairs={{8,0},{16,8},{24,16},{32,24},{40,32},{48,40},{56,48},{64,56},{72,6... | collective-permute-start | bytes 589832 | tf_op jit(solution)/shard_map/ppermute | solution.py:19
  76.8 1.2 copy-start.1
  129.0 7.3 %slice-start = ((s8[6291456]{0:T(1024)(128)(4,1)}), s8[4194304]{0:T(1024)(128)(4,1)S(1)}, s32[]{:S(2)}) async-start(s8[6291456]{0:T(1024)(128)(4,1)} %bitcast.41), calls=%async_computation.2 | async-start | bytes 8388608
  132.6 3.7 slice-start.1
Sparse Core Ops, SparseCore 0:
  66.0 56.5 all-gather.2
  124.7 51.3 all-gather.4
where the time goes:
time: 496 us
  blocking collectives  280 us (56%)
  waiting for transfers between devices  110 us (22%)
  other arithmetic  25.8 us (5%)
  starting transfers between devices  25.5 us (5%)
  matrix products  24.2 us (5%)
  local copies, waits for them, and re-layouts  14.9 us (3%)
  between operations  14.4 us (3%)
    psum x1, blocking collectives, shards(): gram, cross = lax.psum((gram_part, cross_part), 'blk')  280 us
    all_gather x1, waiting for transfers between devices, shards(): lax.all_gather(current, 'mode', axis=0, tiled=True)  43.2 us
    all_gather x1, waiting for transfers between devices, shards(): lax.all_gather(image, 'mode', axis=0, tiled=True)  34.4 us
    ppermute x5, waiting for transfers between devices, extended(): after = lax.ppermute(initial, axis, down)  22.4 us
    ppermute x5, starting transfers between devices, extended(): before = lax.ppermute(last, axis, up)  18.8 us
    ppermute x5, waiting for transfers between devices, extended(): before = lax.ppermute(last, axis, up)  10.1 us
  transfers between devices with their start and end apart: 12, of which 12 were waited for; matrix products, arithmetic and copies ran while one was open for 4% of the time, Pallas kernels for 0%

commit v1 on v0

v1 whole, which is shorter than its diff:
```python
import functools
import math

import jax
import jax.numpy as jnp
from jax import lax
from jax.experimental import pallas as pl
from jax.experimental.pallas import tpu as pltpu
from jax.sharding import PartitionSpec as P

CENTER = 64.0
HALF_WIDTH = 56.0
MASS_SHIFT = 0.5
MESH = pl.DeviceIdType.MESH
HIGH = lax.Precision.HIGHEST
STEPS = 5


def kernel(blks, groups, x_ref, mat_ref, tab_ref, out_ref, proj_ref,
           coef, field, halo_out, halo_in, filt_out, image_out, filt_in, image_in,
           wide, back, part, part_in, tile_y, in_y, tile_z, in_z, tile_all, total,
           halo_send, halo_recv, filt_send, filt_recv, image_send, image_recv,
           back_send, back_recv, sum_send, sum_recv):
    modes, comps, planes, ny, nz = x_ref.shape
    every = modes * groups
    side = math.isqrt(blks)
    blk, me = lax.axis_index("blk"), lax.axis_index("mode")
    left, right = lax.rem(blk + blks - 1, blks), lax.rem(blk + 1, blks)
    my_z, my_y = lax.div(blk, side), lax.rem(blk, side)

    def mode_peer(step):
        return lax.rem(me + step, groups)

    def y_peer(step):
        return my_z * side + lax.rem(my_y + step, side)

    def z_peer(step):
        return lax.rem(my_z + step, side) * side + my_y

    barrier = pltpu.get_barrier_semaphore()

    def greet(to_blk, to_mode):
        pl.semaphore_signal(barrier, inc=1, device_id={"blk": to_blk, "mode": to_mode}, device_id_type=MESH)

    greet(left, me)
    greet(right, me)
    for step in range(1, groups):
        greet(blk, mode_peer(step))
    for step in range(1, side):
        greet(y_peer(step), me)
        greet(z_peer(step), me)

    scale = 2.0 / HALF_WIDTH
    for plane in range(planes):
        labels = mat_ref[plane]
        table = jnp.zeros((ny, nz), jnp.float32)
        for label in range(tab_ref.shape[0]):
            table = jnp.where(labels == label, tab_ref[label], table)
        root = jnp.sqrt(table)
        coef[0, plane] = root
        coef[1, plane] = scale * (27.0 * table + (MASS_SHIFT - CENTER))
        coef[2, plane] = scale * table
        coef[3, plane] = 1.0 / root
        coef[4, plane] = (27.0 * table + MASS_SHIFT) / root
    has_left = jnp.where(blk > 0, 1.0, 0.0).astype(jnp.float32)
    has_right = jnp.where(blk < blks - 1, 1.0, 0.0).astype(jnp.float32)
    top = planes - 1

    rows = lax.broadcasted_iota(jnp.int32, (ny, nz), 0)
    lanes = lax.broadcasted_iota(jnp.int32, (ny, nz), 1)

    def box(w):
        before = jnp.where(rows == 0, 0.0, pltpu.roll(w, 1, 0))
        after = jnp.where(rows == ny - 1, 0.0, pltpu.roll(w, ny - 1, 0))
        w = w + (before + after)
        before = jnp.where(lanes == 0, 0.0, pltpu.roll(w, 1, 1))
        after = jnp.where(lanes == nz - 1, 0.0, pltpu.roll(w, nz - 1, 1))
        return w + (before + after)

    def over_modes(body):
        def run(mode, carry):
            body(mode)
            return carry
        lax.fori_loop(0, modes, run, 0, unroll=2)

    def put(tiles, comp, plane, mode, value):
        for half in range(ny // 8):
            tiles[comp, plane * (ny // 8) + half, pl.ds(pl.multiple_of(mode * 8, 8), 8)] = value[8 * half:8 * half + 8]

    def halos(step, comp):
        return (
            pltpu.make_async_remote_copy(
                src_ref=halo_out.at[step, comp, 0], dst_ref=halo_in.at[step, comp, 1],
                send_sem=halo_send.at[step, comp, 0], recv_sem=halo_recv.at[step, comp, 1],
                device_id={"blk": left, "mode": me}, device_id_type=MESH),
            pltpu.make_async_remote_copy(
                src_ref=halo_out.at[step, comp, 1], dst_ref=halo_in.at[step, comp, 0],
                send_sem=halo_send.at[step, comp, 1], recv_sem=halo_recv.at[step, comp, 0],
                device_id={"blk": right, "mode": me}, device_id_type=MESH),
        )

    def spread(tiles_out, tiles_in, send, recv, comp):
        chunk = modes * 8
        for step in range(1, groups):
            peer = mode_peer(step)
            pltpu.make_async_remote_copy(
                src_ref=tiles_out.at[comp, peer],
                dst_ref=tiles_in.at[comp, pl.ds(pl.multiple_of(me * chunk, chunk), chunk)],
                send_sem=send.at[comp], recv_sem=recv.at[comp],
                device_id={"blk": blk, "mode": peer}, device_id_type=MESH).start()
        tiles_in[comp, pl.ds(pl.multiple_of(me * chunk, chunk), chunk)] = tiles_out[comp, me]

    def spread_wait(tiles_in, send, recv, comp):
        most = tiles_in.at[comp, pl.ds(0, (groups - 1) * modes * 8)]
        pltpu.make_async_copy(most, most, recv.at[comp]).wait()
        pltpu.make_async_copy(most, most, send.at[comp]).wait()

    def edges(step, comp):
        now = step % 2
        factor = 0.5 if step == 1 else 1.0

        def body(mode):
            for slot, plane, has in ((0, 0, has_left), (1, top, has_right)):
                if step == 0:
                    w = coef[0, plane] * x_ref[mode, comp, plane]
                else:
                    w = field[now, comp, plane, mode] - (factor * has) * coef[2, plane] * halo_in[step - 1, comp, slot, mode]
                field[now, comp, plane, mode] = w
                halo_out[step, comp, slot, mode] = box(w)
        over_modes(body)

    def inside(step, comp):
        now, other = step % 2, 1 - step % 2

        def body(mode):
            values, boxes = [], []
            for plane in range(planes):
                if step == 0 and 0 < plane < top:
                    w = coef[0, plane] * x_ref[mode, comp, plane]
                    field[now, comp, plane, mode] = w
                else:
                    w = field[now, comp, plane, mode]
                values.append(w)
                if plane == 0:
                    boxes.append(halo_out[step, comp, 0, mode])
                elif plane == top:
                    boxes.append(halo_out[step, comp, 1, mode])
                else:
                    boxes.append(box(w))
            for plane in range(planes):
                total_box = boxes[plane]
                if plane > 0:
                    total_box = total_box + boxes[plane - 1]
                if plane < top:
                    total_box = total_box + boxes[plane + 1]
                w = values[plane]
                if step == STEPS - 1:
                    put(filt_out, comp, plane, mode, w * coef[3, plane])
                    put(image_out, comp, plane, mode, coef[4, plane] * w - coef[0, plane] * total_box)
                else:
                    new = coef[1, plane] * w - coef[2, plane] * total_box
                    if step == 0:
                        new = 0.5 * new
                    else:
                        new = new - field[other, comp, plane, mode]
                    field[other, comp, plane, mode] = new
        over_modes(body)

    def close(comp):
        def body(mode):
            for slot, plane, has in ((0, 0, has_left), (1, top, has_right)):
                change = has * coef[0, plane] * halo_in[STEPS - 1, comp, slot, mode]
                for half in range(ny // 8):
                    at = (comp, plane * (ny // 8) + half, pl.ds(pl.multiple_of(mode * 8, 8), 8))
                    image_out[at] = image_out[at] - change[8 * half:8 * half + 8]
        over_modes(body)

    greeted = False
    for step in range(STEPS):
        for comp in range(comps):
            if step > 0:
                for copy in halos(step - 1, comp):
                    copy.wait()
            edges(step, comp)
            if not greeted:
                pl.semaphore_wait(barrier, 2 + (groups - 1) + 2 * (side - 1))
                greeted = True
            for copy in halos(step, comp):
                copy.start()
            inside(step, comp)
            if step == STEPS - 1:
                spread(filt_out, filt_in, filt_send, filt_recv, comp)
    for comp in range(comps):
        for copy in halos(STEPS - 1, comp):
            copy.wait()
        close(comp)
        spread(image_out, image_in, image_send, image_recv, comp)

    sums = jnp.zeros((every, 2 * every), jnp.float32)
    for comp in range(comps):
        spread_wait(filt_in, filt_send, filt_recv, comp)
        for row in range(8):
            wide[comp, pl.ds(every, every), pl.ds(row * nz, nz)] = filt_in[comp, pl.ds(row, every, stride=8)]
        spread_wait(image_in, image_send, image_recv, comp)
        for row in range(8):
            wide[comp, pl.ds(0, every), pl.ds(row * nz, nz)] = image_in[comp, pl.ds(row, every, stride=8)]
        both = wide[comp]
        sums = sums + lax.dot_general(both[every:], both, (((1,), (1,)), ((), ())),
                                      precision=HIGH, preferred_element_type=jnp.float32)
    part[...] = sums

    def exchange(phase, count, my_slot, source, target, own, device):
        for step in range(1, count):
            to_blk, to_mode, slot = device(step)
            pltpu.make_async_remote_copy(
                src_ref=source(slot), dst_ref=target.at[my_slot],
                send_sem=sum_send.at[phase], recv_sem=sum_recv.at[phase],
                device_id={"blk": to_blk, "mode": to_mode}, device_id_type=MESH).start()
        target[my_slot] = own
        most = target.at[pl.ds(0, count - 1)]
        pltpu.make_async_copy(most, most, sum_recv.at[phase]).wait()
        pltpu.make_async_copy(most, most, sum_send.at[phase]).wait()

    def added(slots, count):
        result = slots[0]
        for slot in range(1, count):
            result = result + slots[slot]
        return result

    exchange(0, groups, me, lambda slot: part.at[pl.ds(pl.multiple_of(slot * 8, 8), 8)], part_in,
             part[pl.ds(pl.multiple_of(me * 8, 8), 8)], lambda step: (blk, mode_peer(step), mode_peer(step)))
    own = added(part_in, groups)
    tile_y[...] = own
    exchange(1, side, my_y, lambda slot: tile_y, in_y, own, lambda step: (y_peer(step), me, 0))
    own = added(in_y, side)
    tile_z[...] = own
    exchange(2, side, my_z, lambda slot: tile_z, in_z, own, lambda step: (z_peer(step), me, 0))
    own = added(in_z, side)
    tile_all[...] = own
    exchange(3, groups, me, lambda slot: tile_all, total, own, lambda step: (blk, mode_peer(step), 0))

    sums = total[...].reshape((every, 2 * every))
    row_at = lax.broadcasted_iota(jnp.int32, (every, 2 * every), 0)
    lane_at = lax.broadcasted_iota(jnp.int32, (every, 2 * every), 1)
    cross = sums[:, :every]
    work = jnp.where(lane_at < every, jnp.where(lane_at == row_at, 1.0, 0.0), sums)
    blocks = [work[8 * j:8 * j + 8] for j in range(every // 8)]
    sub = lax.broadcasted_iota(jnp.int32, (8, 2 * every), 0)
    for k in range(every):
        j, r = divmod(k, 8)
        row = blocks[j][r:r + 1]
        row = row / row[:, every + k:every + k + 1]
        for i in range(j, every // 8):
            column = blocks[i][:, every + k:every + k + 1]
            change = column * row
            if i == j:
                change = jnp.where(sub > r, change, 0.0)
            blocks[i] = blocks[i] - change
    work = jnp.concatenate(blocks, axis=0)
    diagonal = jnp.sum(jnp.where(lane_at == row_at + every, work, 0.0), axis=1, keepdims=True)
    inverse = (work / jnp.sqrt(diagonal))[:, :every]

    def back_copies(comp):
        half = ny // 8
        for step in range(1, groups):
            peer = mode_peer(step)
            yield pltpu.make_async_remote_copy(
                src_ref=back.at[comp, pl.ds(peer * modes, modes)],
                dst_ref=out_ref.at[:, comp, lax.div(me, half), pl.ds(pl.multiple_of(lax.rem(me, half) * 8, 8), 8)],
                send_sem=back_send.at[comp], recv_sem=back_recv.at[comp],
                device_id={"blk": blk, "mode": peer}, device_id_type=MESH)

    def own_copy(comp):
        half = ny // 8
        return pltpu.make_async_copy(
            back.at[comp, pl.ds(me * modes, modes)],
            out_ref.at[:, comp, lax.div(me, half), pl.ds(pl.multiple_of(lax.rem(me, half) * 8, 8), 8)],
            back_send.at[comps + comp])

    for comp in range(comps):
        result = jnp.dot(inverse, wide[comp, pl.ds(every, every)], precision=HIGH, preferred_element_type=jnp.float32)
        for row in range(8):
            back[comp, :, row] = result[:, row * nz:(row + 1) * nz]
        for copy in back_copies(comp):
            copy.start()
        own_copy(comp).start()
    half = jnp.dot(inverse, cross, precision=HIGH, preferred_element_type=jnp.float32)
    proj_ref[...] = lax.dot_general(half, inverse, (((1,), (1,)), ((), ())), precision=HIGH,
                                    preferred_element_type=jnp.float32)
    for comp in range(comps):
        own_copy(comp).wait()
        most = back.at[comp, pl.ds(0, (groups - 1) * modes)]
        pltpu.make_async_copy(most, most, back_recv.at[comp]).wait()
        pltpu.make_async_copy(most, most, back_send.at[comp]).wait()


def shards(blks, groups, start_modes, materials, stiffness_table):
    modes, comps, planes, ny, nz = start_modes.shape
    every = modes * groups
    side = math.isqrt(blks)
    vmem, dma = pltpu.VMEM, pltpu.SemaphoreType.DMA
    f32 = jnp.float32
    whole = pl.BlockSpec(memory_space=pltpu.VMEM)
    halo = (STEPS, comps, 2, modes, ny, nz)
    tiles_out = (comps, groups, modes * 8, nz)
    tiles_in = (comps, every * 8, nz)
    tile = (8, 2 * every)
    return pl.pallas_call(
        functools.partial(kernel, blks, groups),
        out_shape=(jax.ShapeDtypeStruct(start_modes.shape, f32), jax.ShapeDtypeStruct((every, every), f32)),
        in_specs=[whole, whole, pl.BlockSpec(memory_space=pltpu.SMEM)],
        out_specs=(pl.BlockSpec(memory_space=pl.ANY), whole),
        scratch_shapes=[
            vmem((5, planes, ny, nz), f32),
            vmem((2, comps, planes, modes, ny, nz), f32),
            vmem(halo, f32), vmem(halo, f32),
            vmem(tiles_out, f32), vmem(tiles_out, f32),
            vmem(tiles_in, f32), vmem(tiles_in, f32),
            vmem((comps, 2 * every, 8 * nz), f32),
            vmem((comps, every, 8, nz), f32),
            vmem((every, 2 * every), f32), vmem((groups,) + tile, f32),
            vmem(tile, f32), vmem((side,) + tile, f32),
            vmem(tile, f32), vmem((side,) + tile, f32),
            vmem(tile, f32), vmem((groups,) + tile, f32),
            dma((STEPS, comps, 2)), dma((STEPS, comps, 2)),
            dma((comps,)), dma((comps,)), dma((comps,)), dma((comps,)),
            dma((2 * comps,)), dma((comps,)), dma((4,)), dma((4,)),
        ],
        compiler_params=pltpu.CompilerParams(
            collective_id=0, has_side_effects=True, vmem_limit_bytes=48 * 1024 * 1024),
    )(start_modes, materials, stiffness_table)


def solution(mesh):
    return jax.shard_map(
        functools.partial(shards, mesh.shape["blk"], mesh.shape["mode"]),
        mesh=mesh,
        in_specs=(P("mode", None, "blk", None, None), P("blk", None, None), P()),
        out_specs=(P("mode", None, "blk", None, None), P()),
        check_vma=False,
    )
```

time: 496 us -> 91.7 us (0.18)
  the two profiles are of different devices: /device:TPU:4 before, /device:TPU:1 now
where the time goes in v1:
time: 91.7 us; the launch traced here: 91.5 us
  Pallas kernels  86.8 us (95%)
  local copies, waits for them, and re-layouts  4.03 us (4%)
    pallas_call x1, Pallas kernels, shards(): pl.pallas_call(functools.partial(kernel, blks, groups), out_shape=(jax.Sh...  86.8 us
    unnamed x8, local copies, waits for them, and re-layouts  4.03 us

profile of v1, /device:TPU:1, one launch (start us, length us, event | category | flops | bytes accessed | tf_op | source)
XLA Modules:
  0.0 91.5 jit_solution(6935449777715747722)
XLA Ops:
  0.6 0.0 copy-start
  0.6 1.1 %copy-done = f32[8,3,4,16,128]{4,3,2,1,0:T(8,128)S(1)} copy-done((f32[8,3,4,16,128]{4,3,2,1,0:T(8,128)S(1)}, f32[8,3,4,16,128]{4,3,2,1,0:T(8,128)}, u32[]{:S(2)}) %copy-start) | copy-done | bytes 786456
  1.8 0.0 copy-start.1
  1.8 0.8 copy-done.1
  2.5 0.0 copy-start.2
  2.5 0.7 copy-done.2
  3.2 86.8 %shard_map.50 = (f32[8,3,4,16,128]{4,3,2,1,0:T(8,128)S(1)}, f32[64,64]{1,0:T(8,128)S(1)}) custom-call(f32[8,3,4,16,128]{4,3,2,1,0:T(8,128)S(1)} %copy-done, s32[4,16,128]{2,1,0:T(8,128)S(1)} %copy-done.1, f32[8]{0:T(128)S(1)} %copy-done.2), custom_call_target="tpu_custom_call" | custom-call | tf_op jit(solution)/shard_map/pallas_call | solution.py:308
  90.0 0.9 copy.7
  90.9 0.6 copy.8
Async XLA Ops:
  0.6 1.1 %copy-start = (f32[8,3,4,16,128]{4,3,2,1,0:T(8,128)S(1)}, f32[8,3,4,16,128]{4,3,2,1,0:T(8,128)}, u32[]{:S(2)}) copy-start(f32[8,3,4,16,128]{4,3,2,1,0:T(8,128)} %x_ref.1) | copy-start | bytes 2359300
  1.8 0.8 copy-start.1
  2.5 0.7 copy-start.2

commit v2 on v0

v2 whole, which is shorter than its diff:
```python
import functools
import math

import jax
import jax.numpy as jnp
from jax import lax
from jax.experimental import pallas as pl
from jax.experimental.pallas import tpu as pltpu
from jax.sharding import PartitionSpec as P

CENTER = 64.0
HALF_WIDTH = 56.0
MASS_SHIFT = 0.5
MESH = pl.DeviceIdType.MESH
HIGH = lax.Precision.HIGHEST
DEGREE = 4


def kernel(blks, groups, x_ref, mat_ref, tab_ref, out_ref, proj_ref,
           own, near, mats, table, table_in, coef, close_coef, field, edge_out, edge_in,
           filt_out, image_out, filt_in, image_in,
           back, part, part_in, tile_y, in_y, tile_z, in_z, tile_all, total,
           load, table_send, table_recv, near_send, near_recv, edge_send, edge_recv,
           filt_send, filt_recv, image_send, image_recv,
           back_send, back_recv, sum_send, sum_recv):
    modes, comps, planes, ny, nz = x_ref.shape
    every = modes * groups
    halves = ny // 8
    tiles = planes * halves
    side = math.isqrt(blks)
    blk, me = lax.axis_index("blk"), lax.axis_index("mode")
    left, right = lax.rem(blk + blks - 1, blks), lax.rem(blk + 1, blks)
    my_z, my_y = lax.div(blk, side), lax.rem(blk, side)

    def mode_peer(step):
        return lax.rem(me + step, groups)

    def y_peer(step):
        return my_z * side + lax.rem(my_y + step, side)

    def z_peer(step):
        return lax.rem(my_z + step, side) * side + my_y

    def remote(src, dst, send, recv, to_blk, to_mode):
        return pltpu.make_async_remote_copy(
            src_ref=src, dst_ref=dst, send_sem=send, recv_sem=recv,
            device_id={"blk": to_blk, "mode": to_mode}, device_id_type=MESH)

    barrier = pltpu.get_barrier_semaphore()

    def greet(to_blk, to_mode):
        pl.semaphore_signal(barrier, inc=1, device_id={"blk": to_blk, "mode": to_mode}, device_id_type=MESH)

    greet(left, me)
    greet(right, me)
    for step in range(1, side):
        greet(y_peer(step), me)
        greet(z_peer(step), me)
    for step in range(1, groups):
        greet(blk, mode_peer(step))

    load_mats = pltpu.make_async_copy(mat_ref, mats, load.at[comps])
    load_mats.start()
    load_own = [pltpu.make_async_copy(x_ref.at[:, comp], own.at[comp], load.at[comp]) for comp in range(comps)]
    for copy in load_own:
        copy.start()

    scale = 2.0 / HALF_WIDTH
    has_left = jnp.where(blk > 0, 1.0, 0.0).astype(jnp.float32)
    has_right = jnp.where(blk < blks - 1, 1.0, 0.0).astype(jnp.float32)

    def over_planes(first, count, body, unroll):
        def run(at, carry):
            body(first + at)
            return carry
        lax.fori_loop(0, count, run, 0, unroll=unroll)

    def all_modes(rows):
        return jnp.broadcast_to(rows[:, None, :], (ny, modes, nz))

    def coefficients(values, plane, has):
        root = jnp.sqrt(values)
        coef[0, plane] = all_modes(has * root)
        coef[1, plane] = all_modes(has * (scale * (27.0 * values + (MASS_SHIFT - CENTER))))
        coef[2, plane] = all_modes(has * (scale * values))
        return root

    load_mats.wait()

    def own_coefficients(plane):
        labels = mats[plane]
        values = jnp.zeros((ny, nz), jnp.float32)
        for label in range(tab_ref.shape[0]):
            values = jnp.where(labels == label, tab_ref[label], values)
        table[plane] = values
        root = coefficients(values, planes + plane, 1.0)
        close_coef[0, plane] = all_modes(1.0 / root)
        close_coef[1, plane] = all_modes((27.0 * values + MASS_SHIFT) / root)

    over_planes(0, planes, own_coefficients, 1)
    pl.semaphore_wait(barrier, 2 + (groups - 1) + 2 * (side - 1))

    to_sides = ((left, 1), (right, 0))
    table_copies = [remote(table, table_in.at[slot], table_send.at[slot], table_recv.at[slot], to, me)
                    for to, slot in to_sides]
    near_copies = [[remote(x_ref.at[:, comp], near.at[slot, comp], near_send.at[slot, comp], near_recv.at[slot, comp], to, me)
                    for to, slot in to_sides] for comp in range(comps)]
    edge_copies = [[remote(edge_out.at[comp, slot, pl.ds(0, 9 - slot)], edge_in.at[comp, slot, pl.ds(0, 9 - slot)],
                           edge_send.at[comp, slot], edge_recv.at[comp, slot], to, me)
                    for to, slot in to_sides] for comp in range(comps)]

    def start(copies):
        for copy in copies:
            copy.start()

    def finish(copies):
        for copy in copies:
            copy.wait()

    start(table_copies)
    start(near_copies[0])
    start(near_copies[1])
    finish(table_copies)

    def near_coefficients(plane):
        coefficients(table_in[0, plane], plane, has_left)
        coefficients(table_in[1, plane], 2 * planes + plane, has_right)

    over_planes(0, planes, near_coefficients, 1)

    lanes = lax.broadcasted_iota(jnp.int32, (ny, modes, nz), 2)
    none = jnp.zeros((1, modes, nz), jnp.float32)

    def box(u):
        v = u + (jnp.concatenate([none, u[:-1]], axis=0) + jnp.concatenate([u[1:], none], axis=0))
        before = jnp.where(lanes == 0, 0.0, pltpu.roll(v, 1, 2))
        after = jnp.where(lanes == nz - 1, 0.0, pltpu.roll(v, nz - 1, 2))
        return v + (before + after)

    def weigh(source, first):
        rows = source.reshape(modes * planes * ny, nz)

        def body(plane):
            for y in range(ny):
                field[0, first + plane, y] = coef[0, first + plane, y] * rows[pl.ds(plane * ny + y, modes, stride=planes * ny)]
        over_planes(0, planes, body, 1)

    def advance(step):
        now, other = step % 2, 1 - step % 2
        first = step + 1

        def body(plane):
            w = field[now, plane]
            u = field[now, plane - 1] + w + field[now, plane + 1]
            new = coef[1, plane] * w - coef[2, plane] * box(u)
            if step == 0:
                new = 0.5 * new
            else:
                new = new - field[other, plane]
            field[other, plane] = new
        over_planes(first, 3 * planes - 2 * first, body, 2)

    def tiles_of(target, comp, plane, value):
        for half in range(halves):
            target[comp, plane * halves + half] = value[8 * half:8 * half + 8]

    def finals(comp):
        first, last = field[0, planes], field[0, 2 * planes - 1]
        edge_out[comp, 1, :8] = box(first)[:8]
        lower = jnp.concatenate([jnp.zeros((8, modes, nz), jnp.float32), last[8:]], axis=0)
        edge_out[comp, 0] = box(lower)[7:]
        start(edge_copies[comp])
        for plane in range(planes):
            w = field[0, planes + plane]
            u = w
            if plane > 0:
                u = u + field[0, planes + plane - 1]
            if plane < planes - 1:
                u = u + field[0, planes + plane + 1]
            tiles_of(filt_out, comp, plane, w * close_coef[0, plane])
            tiles_of(image_out, comp, plane, close_coef[1, plane] * w - coef[0, planes + plane] * box(u))

    def spread(source, target, send, recv, comp, peer):
        remote(source.at[comp, peer], target.at[comp, :, pl.ds(pl.multiple_of(me * modes, modes), modes)],
               send.at[comp], recv.at[comp], blk, peer).start()

    def keep(source, target, comp):
        target[comp, :, pl.ds(pl.multiple_of(me * modes, modes), modes)] = source[comp, me]

    late = (0, 1, tiles - halves)

    def spread_early(comp):
        for step in range(1, groups):
            spread(filt_out, filt_in, filt_send, filt_recv, comp, mode_peer(step))
        for step in range(1, groups):
            peer = mode_peer(step)

            @pl.when((peer != late[0]) & (peer != late[1]) & (peer != late[2]))
            def _():
                spread(image_out, image_in, image_send, image_recv, comp, peer)
        keep(filt_out, filt_in, comp)

    def spread_late(comp):
        finish(edge_copies[comp])
        twice_left, twice_right = 2.0 * has_left, 2.0 * has_right
        image_out[comp, 0, 7] = image_out[comp, 0, 7] - twice_left * coef[0, planes, 7] * edge_in[comp, 0, 0]
        image_out[comp, 1] = image_out[comp, 1] - twice_left * coef[0, planes, pl.ds(8, 8)] * edge_in[comp, 0, pl.ds(1, 8)]
        image_out[comp, late[2]] = (image_out[comp, late[2]]
                                    - twice_right * coef[0, 2 * planes - 1, pl.ds(0, 8)] * edge_in[comp, 1, pl.ds(0, 8)])
        for tile in late:
            @pl.when(me != tile)
            def _():
                spread(image_out, image_in, image_send, image_recv, comp, tile)
        keep(image_out, image_in, comp)

    def spread_wait(target, send, recv, comp):
        most = target.at[comp, :, pl.ds(0, (groups - 1) * modes)]
        pltpu.make_async_copy(most, most, recv.at[comp]).wait()
        pltpu.make_async_copy(most, most, send.at[comp]).wait()

    for comp in range(comps):
        load_own[comp].wait()
        weigh(own.at[comp], planes)
        finish(near_copies[comp])
        weigh(near.at[0, comp], 0)
        weigh(near.at[1, comp], 2 * planes)
        for step in range(DEGREE):
            advance(step)
        finals(comp)
        if comp + 2 < comps:
            start(near_copies[comp + 2])
        spread_early(comp)
        if comp > 0:
            spread_late(comp - 1)

    def add_sums(sums, comp):
        spread_wait(filt_in, filt_send, filt_recv, comp)
        spread_wait(image_in, image_send, image_recv, comp)
        for row in range(0, 8, 2):
            filt = jnp.concatenate([filt_in[comp, row], filt_in[comp, row + 1]], axis=1)
            image = jnp.concatenate([image_in[comp, row], image_in[comp, row + 1]], axis=1)
            sums = sums + lax.dot_general(filt, jnp.concatenate([image, filt], axis=0), (((1,), (1,)), ((), ())),
                                          precision=HIGH, preferred_element_type=jnp.float32)
        return sums

    sums = jnp.zeros((every, 2 * every), jnp.float32)
    for comp in range(comps - 1):
        sums = add_sums(sums, comp)
    spread_late(comps - 1)
    part[...] = add_sums(sums, comps - 1)

    def exchange(phase, count, my_slot, source, target, own_tile, device):
        for step in range(1, count):
            to_blk, to_mode, slot = device(step)
            remote(source(slot), target.at[my_slot], sum_send.at[phase], sum_recv.at[phase], to_blk, to_mode).start()
        target[my_slot] = own_tile
        most = target.at[pl.ds(0, count - 1)]
        pltpu.make_async_copy(most, most, sum_recv.at[phase]).wait()
        pltpu.make_async_copy(most, most, sum_send.at[phase]).wait()

    def added(slots, count):
        result = slots[0]
        for slot in range(1, count):
            result = result + slots[slot]
        return result

    exchange(0, groups, me, lambda slot: part.at[pl.ds(pl.multiple_of(slot * 8, 8), 8)], part_in,
             part[pl.ds(pl.multiple_of(me * 8, 8), 8)], lambda step: (blk, mode_peer(step), mode_peer(step)))
    tile = added(part_in, groups)
    tile_y[...] = tile
    exchange(1, side, my_y, lambda slot: tile_y, in_y, tile, lambda step: (y_peer(step), me, 0))
    tile = added(in_y, side)
    tile_z[...] = tile
    exchange(2, side, my_z, lambda slot: tile_z, in_z, tile, lambda step: (z_peer(step), me, 0))
    tile = added(in_z, side)
    tile_all[...] = tile
    exchange(3, groups, me, lambda slot: tile_all, total, tile, lambda step: (blk, mode_peer(step), 0))

    sums = total[...].reshape((every, 2 * every))
    row_at = lax.broadcasted_iota(jnp.int32, (every, 2 * every), 0)
    lane_at = lax.broadcasted_iota(jnp.int32, (every, 2 * every), 1)
    cross = sums[:, :every]
    work = jnp.where(lane_at < every, jnp.where(lane_at == row_at, 1.0, 0.0), sums)
    blocks = [work[8 * j:8 * j + 8] for j in range(every // 8)]
    sub = lax.broadcasted_iota(jnp.int32, (8, 2 * every), 0)
    for k in range(every):
        j, r = divmod(k, 8)
        row = blocks[j][r:r + 1]
        row = row / row[:, every + k:every + k + 1]
        for i in range(j, every // 8):
            column = blocks[i][:, every + k:every + k + 1]
            change = column * row
            if i == j:
                change = jnp.where(sub > r, change, 0.0)
            blocks[i] = blocks[i] - change
    work = jnp.concatenate(blocks, axis=0)
    diagonal = jnp.sum(jnp.where(lane_at == row_at + every, work, 0.0), axis=1, keepdims=True)
    inverse = (work / jnp.sqrt(diagonal))[:, :every]

    def place():
        return lax.div(me, halves), pl.ds(pl.multiple_of(lax.rem(me, halves) * 8, 8), 8)

    def back_copies(comp):
        plane, rows = place()
        return [remote(back.at[comp, pl.ds(mode_peer(step) * modes, modes)], out_ref.at[:, comp, plane, rows],
                       back_send.at[comp], back_recv.at[comp], blk, mode_peer(step)) for step in range(1, groups)]

    def own_copy(comp):
        plane, rows = place()
        return pltpu.make_async_copy(back.at[comp, pl.ds(me * modes, modes)], out_ref.at[:, comp, plane, rows],
                                     back_send.at[comps + comp])

    for comp in range(comps):
        filt = jnp.concatenate([filt_in[comp, row] for row in range(8)], axis=1)
        result = jnp.dot(inverse, filt, precision=HIGH, preferred_element_type=jnp.float32)
        for row in range(8):
            back[comp, :, row] = result[:, row * nz:(row + 1) * nz]
        start(back_copies(comp))
        own_copy(comp).start()
    half = jnp.dot(inverse, cross, precision=HIGH, preferred_element_type=jnp.float32)
    product = lax.dot_general(half, inverse, (((1,), (1,)), ((), ())), precision=HIGH,
                              preferred_element_type=jnp.float32)
    proj_ref[...] = 0.5 * (product + product.T)
    for comp in range(comps):
        own_copy(comp).wait()
        most = back.at[comp, pl.ds(0, (groups - 1) * modes)]
        pltpu.make_async_copy(most, most, back_recv.at[comp]).wait()
        pltpu.make_async_copy(most, most, back_send.at[comp]).wait()


def shards(blks, groups, start_modes, materials, stiffness_table):
    modes, comps, planes, ny, nz = start_modes.shape
    every = modes * groups
    side = math.isqrt(blks)
    vmem, dma = pltpu.VMEM, pltpu.SemaphoreType.DMA
    f32 = jnp.float32
    slab = (modes, planes, ny, nz)
    edge = (comps, 2, 9, modes, nz)
    tiles_out = (comps, groups, 8, modes, nz)
    tiles_in = (comps, 8, every, nz)
    tile = (8, 2 * every)
    return pl.pallas_call(
        functools.partial(kernel, blks, groups),
        out_shape=(jax.ShapeDtypeStruct(start_modes.shape, f32), jax.ShapeDtypeStruct((every, every), f32)),
        in_specs=[pl.BlockSpec(memory_space=pl.ANY), pl.BlockSpec(memory_space=pl.ANY), pl.BlockSpec(memory_space=pltpu.SMEM)],
        out_specs=(pl.BlockSpec(memory_space=pl.ANY), pl.BlockSpec(memory_space=pltpu.VMEM)),
        scratch_shapes=[
            vmem((comps,) + slab, f32), vmem((2, comps) + slab, f32),
            vmem((planes, ny, nz), jnp.int32), vmem((planes, ny, nz), f32), vmem((2, planes, ny, nz), f32),
            vmem((3, 3 * planes, ny, modes, nz), f32), vmem((2, planes, ny, modes, nz), f32),
            vmem((2, 3 * planes, ny, modes, nz), f32),
            vmem(edge, f32), vmem(edge, f32),
            vmem(tiles_out, f32), vmem(tiles_out, f32),
            vmem(tiles_in, f32), vmem(tiles_in, f32),
            vmem((comps, every, 8, nz), f32),
            vmem((every, 2 * every), f32), vmem((groups,) + tile, f32),
            vmem(tile, f32), vmem((side,) + tile, f32),
            vmem(tile, f32), vmem((side,) + tile, f32),
            vmem(tile, f32), vmem((groups,) + tile, f32),
            dma((comps + 1,)), dma((2,)), dma((2,)),
            dma((2, comps)), dma((2, comps)), dma((comps, 2)), dma((comps, 2)),
            dma((comps,)), dma((comps,)), dma((comps,)), dma((comps,)),
            dma((2 * comps,)), dma((comps,)), dma((4,)), dma((4,)),
        ],
        compiler_params=pltpu.CompilerParams(
            collective_id=0, has_side_effects=True, vmem_limit_bytes=60 * 1024 * 1024),
    )(start_modes, materials, stiffness_table)


def solution(mesh):
    return jax.shard_map(
        functools.partial(shards, mesh.shape["blk"], mesh.shape["mode"]),
        mesh=mesh,
        in_specs=(P("mode", None, "blk", None, None), P("blk", None, None), P()),
        out_specs=(P("mode", None, "blk", None, None), P()),
        check_vma=False,
    )
```

time: 496 us -> 88.8 us (0.18)
  the two profiles are of different devices: /device:TPU:4 before, /device:TPU:1 now
where the time goes in v2:
time: 88.8 us; the launch traced here: 88.7 us
  Pallas kernels  85.3 us (96%)
  local copies, waits for them, and re-layouts  2.71 us (3%)
    pallas_call x1, Pallas kernels, shards(): pl.pallas_call(functools.partial(kernel, blks, groups), out_shape=(jax.Sh...  85.3 us
    unnamed x4, local copies, waits for them, and re-layouts  2.71 us

profile of v2, /device:TPU:1, one launch (start us, length us, event | category | flops | bytes accessed | tf_op | source)
XLA Modules:
  0.0 88.7 jit_solution(3466479133407497113)
XLA Ops:
  0.6 85.3 %shard_map.50 = (f32[8,3,4,16,128]{4,3,2,1,0:T(8,128)}, f32[64,64]{1,0:T(8,128)}) custom-call(f32[8,3,4,16,128]{4,3,2,1,0:T(8,128)} %x_ref.1, s32[4,16,128]{2,1,0:T(8,128)} %mat_ref.1, f32[8]{0:T(128)} %tab_ref.1), custom_call_target="tpu_custom_call" | custom-call | tf_op jit(solution)/shard_map/pallas_call | solution.py:342
  86.0 0.0 copy-start
  86.0 2.1 %copy.7 = f32[8,3,4,16,128]{4,3,2,1,0:T(8,128)} copy(f32[8,3,4,16,128]{4,3,2,1,0:T(8,128)} %get-tuple-element.4) | data formatting | bytes 1572864
  88.1 0.0 copy-done
  88.1 0.6 copy.8
Async XLA Ops:
  86.0 2.1 %copy-start = (f32[64,64]{1,0:T(8,128)S(1)}, f32[64,64]{1,0:T(8,128)}, u32[]{:S(2)}) copy-start(f32[64,64]{1,0:T(8,128)} %get-tuple-element.5) | copy-start | bytes 49156

commit v3 on v2

v3 whole, which is shorter than its diff:
```python
import functools
import math

import jax
import jax.numpy as jnp
from jax import lax
from jax.experimental import pallas as pl
from jax.experimental.pallas import tpu as pltpu
from jax.sharding import PartitionSpec as P

CENTER = 64.0
HALF_WIDTH = 56.0
MASS_SHIFT = 0.5
MESH = pl.DeviceIdType.MESH
HIGH = lax.Precision.HIGHEST
DEGREE = 4


def kernel(blks, groups, x_ref, mat_ref, tab_hbm, out_ref, proj_ref,
           tab_ref, own, mats, table, table_in, coef, close, field, odd, edge_out, edge_in,
           filt_out, image_out, filt_in, image_in,
           back, part, part_in, tile_y, in_y, tile_z, in_z, tile_all, total,
           load, table_send, table_recv, near_send, near_recv, edge_send, edge_recv,
           filt_send, filt_recv, image_send, image_recv,
           back_send, back_recv, sum_send, sum_recv):
    modes, comps, planes, ny, nz = x_ref.shape
    every = modes * groups
    halves = ny // 8
    side = math.isqrt(blks)
    blk, me = lax.axis_index("blk"), lax.axis_index("mode")
    left, right = lax.rem(blk + blks - 1, blks), lax.rem(blk + 1, blks)
    my_z, my_y = lax.div(blk, side), lax.rem(blk, side)
    no_left, no_right = blk == 0, blk == blks - 1

    def mode_peer(step):
        return lax.rem(me + step, groups)

    def y_peer(step):
        return my_z * side + lax.rem(my_y + step, side)

    def z_peer(step):
        return lax.rem(my_z + step, side) * side + my_y

    def tile_of(device):
        return lax.rem(device, 2) * 4 + lax.rem(lax.div(device, 2), 2) * 2 + lax.div(device, 4)

    my_tile = tile_of(me)

    def remote(src, dst, send, recv, to_blk, to_mode):
        return pltpu.make_async_remote_copy(
            src_ref=src, dst_ref=dst, send_sem=send, recv_sem=recv,
            device_id={"blk": to_blk, "mode": to_mode}, device_id_type=MESH)

    def arrived(ref, semaphore):
        pltpu.make_async_copy(ref, ref, semaphore).wait()

    owner_last, owner_first, owner_row = 3, 4, 0

    barrier = pltpu.get_barrier_semaphore()

    def greet(to_blk, to_mode):
        pl.semaphore_signal(barrier, inc=1, device_id={"blk": to_blk, "mode": to_mode}, device_id_type=MESH)

    greet(left, me)
    greet(right, me)
    for step in range(1, side):
        greet(y_peer(step), me)
        greet(z_peer(step), me)
    for step in range(1, groups):
        greet(blk, mode_peer(step))

    @pl.when(me == owner_last)
    def _():
        for mode in range(groups):
            greet(right, mode)

    @pl.when((me == owner_first) | (me == owner_row))
    def _():
        for mode in range(groups):
            greet(left, mode)

    load_mats = pltpu.make_async_copy(mat_ref, mats, load.at[comps])
    load_mats.start()
    load_tab = pltpu.make_async_copy(tab_hbm, tab_ref, load.at[comps + 1])
    load_tab.start()

    def load_own(comp):
        return pltpu.make_async_copy(x_ref.at[:, comp], own.at[comp], load.at[comp])

    for comp in range(comps):
        load_own(comp).start()

    def over(count, body, unroll=1):
        def run(at, carry):
            body(at)
            return carry
        lax.fori_loop(0, count, run, 0, unroll=unroll)

    @pl.when(no_left)
    def _():
        table_in[0] = jnp.zeros_like(table)

        def clear(plane):
            for comp in range(comps):
                field[comp, plane] = jnp.zeros((ny, modes, nz), jnp.float32)
        over(planes, clear)

    @pl.when(no_right)
    def _():
        table_in[1] = jnp.zeros_like(table)

        def clear(plane):
            for comp in range(comps):
                field[comp, 2 * planes + plane] = jnp.zeros((ny, modes, nz), jnp.float32)
        over(planes, clear)

    scale = 2.0 / HALF_WIDTH

    def all_modes(rows):
        return jnp.broadcast_to(rows[:, None, :], (ny, modes, nz))

    def coefficients(values, plane):
        coef[0, plane] = all_modes(scale * (27.0 * values + (MASS_SHIFT - CENTER)))
        coef[1, plane] = all_modes(scale * values)

    load_mats.wait()
    load_tab.wait()

    def own_root(plane):
        labels = mats[plane]
        values = jnp.zeros((ny, nz), jnp.float32)
        for label in range(tab_ref.shape[0]):
            values = jnp.where(labels == label, tab_ref[label], values)
        table[plane] = values
        close[0, plane] = all_modes(jnp.sqrt(values))

    over(planes, own_root)

    def weigh(comp):
        load_own(comp).wait()
        rows = own.at[comp].reshape(modes * planes * ny, nz)

        def body(plane):
            for y in range(ny):
                field[comp, planes + plane, y] = close[0, plane, y] * rows[pl.ds(plane * ny + y, modes, stride=planes * ny)]
        over(planes, body)

    weigh(0)
    pl.semaphore_wait(barrier, 5 + (groups - 1) + 2 * (side - 1))

    def table_copy(slot):
        return remote(table, table_in.at[slot], table_send.at[slot], table_recv.at[slot], (right, left)[slot], me)

    def near_copy(comp, slot):
        return remote(field.at[comp, pl.ds(planes, planes)], field.at[comp, pl.ds(2 * planes * slot, planes)],
                      near_send.at[slot, comp], near_recv.at[slot, comp], (right, left)[slot], me)

    def edge_copies(comp):
        mine = pl.ds(pl.multiple_of(me * modes, modes), modes)
        to_left = [remote(edge_out.at[comp, 1, pl.ds(0, 8)], edge_in.at[comp, :, mine],
                          edge_send.at[comp, 0], edge_recv.at[comp], left, owner_last)]
        to_right = [remote(edge_out.at[comp, 0, pl.ds(1, 8)], edge_in.at[comp, :, mine],
                           edge_send.at[comp, 1], edge_recv.at[comp], right, owner_first),
                    remote(edge_out.at[comp, 0, pl.ds(0, 1)], edge_in.at[comp, pl.ds(0, 1), mine],
                           edge_send.at[comp, 2], edge_recv.at[comp], right, owner_row)]
        return to_left, to_right

    @pl.when(jnp.logical_not(no_left))
    def _():
        table_copy(1).start()
        near_copy(0, 1).start()

    @pl.when(jnp.logical_not(no_right))
    def _():
        table_copy(0).start()
        near_copy(0, 0).start()

    for comp in range(1, comps):
        weigh(comp)

        @pl.when(jnp.logical_not(no_left))
        def _():
            near_copy(comp, 1).start()

        @pl.when(jnp.logical_not(no_right))
        def _():
            near_copy(comp, 0).start()

    def own_coefficients(plane):
        values = table[plane]
        coefficients(values, planes + plane)
        root = jnp.sqrt(values)
        close[1, plane] = all_modes(1.0 / root)
        close[2, plane] = all_modes((27.0 * values + MASS_SHIFT) / root)

    over(planes, own_coefficients)

    @pl.when(jnp.logical_not(no_left))
    def _():
        table_copy(0).wait_recv()
        table_copy(1).wait_send()

    @pl.when(jnp.logical_not(no_right))
    def _():
        table_copy(1).wait_recv()
        table_copy(0).wait_send()

    def near_coefficients(plane):
        coefficients(table_in[0, plane], plane)
        coefficients(table_in[1, plane], 2 * planes + plane)

    over(planes, near_coefficients)

    none = jnp.zeros((1, modes, nz), jnp.float32)

    def box_z(v):
        lanes = lax.broadcasted_iota(jnp.int32, v.shape, 2)
        before = jnp.where(lanes == 0, 0.0, pltpu.roll(v, 1, 2))
        after = jnp.where(lanes == nz - 1, 0.0, pltpu.roll(v, nz - 1, 2))
        return v + (before + after)

    def box(u):
        return box_z(u + (jnp.concatenate([none, u[:-1]], axis=0) + jnp.concatenate([u[1:], none], axis=0)))

    def advance(step, comp):
        even = field.at[comp]
        now, other = (even, odd) if step % 2 == 0 else (odd, even)
        first = step + 1

        def body(at):
            plane = first + at
            w = now[plane]
            u = now[plane - 1] + w + now[plane + 1]
            new = coef[0, plane] * w - coef[1, plane] * box(u)
            if step == 0:
                new = 0.5 * new
            else:
                new = new - other[plane]
            other[plane] = new
        over(3 * planes - 2 * first, body, 2)

    def finals(comp):
        first, last = field[comp, planes, :9], field[comp, 2 * planes - 1, 8:]
        edge_out[comp, 1, :8] = box_z(first[:8] + (first[1:] + jnp.concatenate([none, first[:7]], axis=0)))
        edge_out[comp, 0] = box_z(jnp.concatenate([none, last], axis=0) + (
            jnp.concatenate([last, none], axis=0) + jnp.concatenate([none, none, last[:-1]], axis=0)))
        to_left, to_right = edge_copies(comp)

        @pl.when(jnp.logical_not(no_left))
        def _():
            for copy in to_left:
                copy.start()

        @pl.when(jnp.logical_not(no_right))
        def _():
            for copy in to_right:
                copy.start()

        field[comp, planes - 1] = jnp.zeros((ny, modes, nz), jnp.float32)
        field[comp, 2 * planes] = jnp.zeros((ny, modes, nz), jnp.float32)

        def body(plane):
            at = planes + plane
            w = field[comp, at]
            filt = w * close[1, plane]
            image = close[2, plane] * w - close[0, plane] * box(field[comp, at - 1] + w + field[comp, at + 1])
            for half in range(halves):
                filt_out[comp, plane * halves + half] = filt[8 * half:8 * half + 8]
                image_out[comp, plane * halves + half] = image[8 * half:8 * half + 8]
        over(planes, body, 2)

    def my_modes():
        return pl.ds(pl.multiple_of(me * modes, modes), modes)

    def spread(source, target, send, recv, comp):
        for step in range(1, groups):
            peer = mode_peer(step)
            remote(source.at[comp, tile_of(peer)], target.at[comp, :, my_modes()],
                   send.at[comp], recv.at[comp], blk, peer).start()

    def spread_wait(target, send, recv, comp):
        most = target.at[comp, :, pl.ds(0, (groups - 1) * modes)]
        arrived(most, recv.at[comp])
        arrived(most, send.at[comp])

    def filter_one(comp):
        @pl.when(jnp.logical_not(no_left))
        def _():
            near_copy(comp, 0).wait_recv()
            near_copy(comp, 1).wait_send()

        @pl.when(jnp.logical_not(no_right))
        def _():
            near_copy(comp, 1).wait_recv()
            near_copy(comp, 0).wait_send()

        for step in range(DEGREE):
            advance(step, comp)
        finals(comp)
        spread(filt_out, filt_in, filt_send, filt_recv, comp)
        spread(image_out, image_in, image_send, image_recv, comp)
        filt_in[comp, :, my_modes()] = filt_out[comp, my_tile]
        image_in[comp, :, my_modes()] = image_out[comp, my_tile]

    over(comps, filter_one)

    def add_edges(comp):
        @pl.when((me == owner_last) & jnp.logical_not(no_right))
        def _():
            arrived(edge_in.at[comp], edge_recv.at[comp])
            for group in range(groups):
                at = pl.ds(group * modes, modes)
                image_in[comp, :, at] = image_in[comp, :, at] - (2.0 * close[0, planes - 1, :8]) * edge_in[comp, :, at]

        @pl.when((me == owner_first) & jnp.logical_not(no_left))
        def _():
            arrived(edge_in.at[comp], edge_recv.at[comp])
            for group in range(groups):
                at = pl.ds(group * modes, modes)
                image_in[comp, :, at] = image_in[comp, :, at] - (2.0 * close[0, 0, 8:]) * edge_in[comp, :, at]

        @pl.when((me == owner_row) & jnp.logical_not(no_left))
        def _():
            arrived(edge_in.at[comp, pl.ds(0, 1)], edge_recv.at[comp])
            for group in range(groups):
                at = pl.ds(group * modes, modes)
                image_in[comp, 7, at] = image_in[comp, 7, at] - (2.0 * close[0, 0, 7]) * edge_in[comp, 0, at]

    part[...] = jnp.zeros_like(part)

    def add_sums(comp):
        spread_wait(filt_in, filt_send, filt_recv, comp)
        spread_wait(image_in, image_send, image_recv, comp)
        add_edges(comp)
        sums = part[...]
        for row in range(0, 8, 2):
            filt = jnp.concatenate([filt_in[comp, row], filt_in[comp, row + 1]], axis=1)
            image = jnp.concatenate([image_in[comp, row], image_in[comp, row + 1]], axis=1)
            sums = sums + lax.dot_general(filt, jnp.concatenate([image, filt], axis=0), (((1,), (1,)), ((), ())),
                                          precision=HIGH, preferred_element_type=jnp.float32)
        part[...] = sums

    over(comps, add_sums)

    def exchange(phase, count, my_slot, source, target, own_tile, device):
        for step in range(1, count):
            to_blk, to_mode, slot = device(step)
            remote(source(slot), target.at[my_slot], sum_send.at[phase], sum_recv.at[phase], to_blk, to_mode).start()
        target[my_slot] = own_tile
        most = target.at[pl.ds(0, count - 1)]
        arrived(most, sum_recv.at[phase])
        arrived(most, sum_send.at[phase])

    def added(slots, count):
        result = slots[0]
        for slot in range(1, count):
            result = result + slots[slot]
        return result

    exchange(0, groups, me, lambda slot: part.at[pl.ds(pl.multiple_of(slot * 8, 8), 8)], part_in,
             part[pl.ds(pl.multiple_of(me * 8, 8), 8)], lambda step: (blk, mode_peer(step), mode_peer(step)))
    tile = added(part_in, groups)
    tile_y[...] = tile
    exchange(1, side, my_y, lambda slot: tile_y, in_y, tile, lambda step: (y_peer(step), me, 0))
    tile = added(in_y, side)
    tile_z[...] = tile
    exchange(2, side, my_z, lambda slot: tile_z, in_z, tile, lambda step: (z_peer(step), me, 0))
    tile = added(in_z, side)
    tile_all[...] = tile
    exchange(3, groups, me, lambda slot: tile_all, total, tile, lambda step: (blk, mode_peer(step), 0))

    sums = total[...].reshape((every, 2 * every))
    row_at = lax.broadcasted_iota(jnp.int32, (every, 2 * every), 0)
    lane_at = lax.broadcasted_iota(jnp.int32, (every, 2 * every), 1)
    cross = sums[:, :every]
    work = jnp.where(lane_at < every, jnp.where(lane_at == row_at, 1.0, 0.0), sums)
    blocks = [work[8 * j:8 * j + 8] for j in range(every // 8)]
    sub = lax.broadcasted_iota(jnp.int32, (8, 2 * every), 0)

    def column(block, lane):
        return jnp.take_along_axis(block, jnp.full((8, 2 * every), lane, jnp.int32), axis=1)

    def spread_row(block, row):
        return jnp.broadcast_to(block[row:row + 1], (8, 2 * every))

    for k in range(0, every, 2):
        j, r = divmod(k, 8)
        ones = [column(block, every + k) for block in blocks[j:]]
        twos = [column(block, every + k + 1) for block in blocks[j:]]
        row_one, row_two = spread_row(blocks[j], r), spread_row(blocks[j], r + 1)
        mixed = spread_row(ones[0], r + 1)
        over_one = 1.0 / spread_row(ones[0], r)
        factor = mixed * over_one
        over_two = 1.0 / (spread_row(twos[0], r + 1) - factor * mixed)
        new_two = row_two - factor * row_one
        scaled_one, scaled_two = row_one * over_one, new_two * over_two
        for i in range(j, every // 8):
            one, two = ones[i - j], twos[i - j]
            less = blocks[i] - (one * scaled_one + (two - one * factor) * scaled_two)
            if i == j:
                less = jnp.where(sub > r + 1, less, jnp.where(sub == r + 1, new_two, blocks[i]))
            blocks[i] = less
    work = jnp.concatenate(blocks, axis=0)
    diagonal = jnp.sum(jnp.where(lane_at == row_at + every, work, 0.0), axis=1, keepdims=True)
    inverse = (work / jnp.sqrt(diagonal))[:, :every]

    def place():
        return lax.div(my_tile, halves), pl.ds(pl.multiple_of(lax.rem(my_tile, halves) * 8, 8), 8)

    def back_copies(comp):
        plane, rows = place()
        return [remote(back.at[comp, pl.ds(mode_peer(step) * modes, modes)], out_ref.at[:, comp, plane, rows],
                       back_send.at[comp], back_recv.at[comp], blk, mode_peer(step)) for step in range(1, groups)]

    def own_copy(comp):
        plane, rows = place()
        return pltpu.make_async_copy(back.at[comp, pl.ds(me * modes, modes)], out_ref.at[:, comp, plane, rows],
                                     back_send.at[comps + comp])

    def give_back(comp):
        filt = jnp.concatenate([filt_in[comp, row] for row in range(8)], axis=1)
        result = jnp.dot(inverse, filt, precision=HIGH, preferred_element_type=jnp.float32)
        for row in range(8):
            back[comp, :, row] = result[:, row * nz:(row + 1) * nz]
        for copy in back_copies(comp):
            copy.start()
        own_copy(comp).start()

    for comp in range(comps):
        give_back(comp)
    half = jnp.dot(inverse, cross, precision=HIGH, preferred_element_type=jnp.float32)
    product = lax.dot_general(half, inverse, (((1,), (1,)), ((), ())), precision=HIGH,
                              preferred_element_type=jnp.float32)
    proj_ref[...] = 0.5 * (product + product.T)

    def finish(comp):
        to_left, to_right = edge_copies(comp)

        @pl.when(jnp.logical_not(no_left))
        def _():
            for copy in to_left:
                copy.wait_send()

        @pl.when(jnp.logical_not(no_right))
        def _():
            for copy in to_right:
                copy.wait_send()

        own_copy(comp).wait()
        most = back.at[comp, pl.ds(0, (groups - 1) * modes)]
        arrived(most, back_recv.at[comp])
        arrived(most, back_send.at[comp])

    over(comps, finish)


def shards(blks, groups, start_modes, materials, stiffness_table):
    modes, comps, planes, ny, nz = start_modes.shape
    every = modes * groups
    side = math.isqrt(blks)
    vmem, dma = pltpu.VMEM, pltpu.SemaphoreType.DMA
    f32 = jnp.float32
    plane = (ny, modes, nz)
    tiles_out = (comps, groups, 8, modes, nz)
    tiles_in = (comps, 8, every, nz)
    tile = (8, 2 * every)
    return pl.pallas_call(
        functools.partial(kernel, blks, groups),
        out_shape=(jax.ShapeDtypeStruct(start_modes.shape, f32), jax.ShapeDtypeStruct((every, every), f32)),
        in_specs=[pl.BlockSpec(memory_space=pltpu.HBM), pl.BlockSpec(memory_space=pltpu.HBM),
                  pl.BlockSpec(memory_space=pltpu.HBM)],
        out_specs=(pl.BlockSpec(memory_space=pl.ANY), pl.BlockSpec(memory_space=pltpu.VMEM)),
        scratch_shapes=[
            pltpu.SMEM(stiffness_table.shape, f32),
            vmem((comps, modes, planes, ny, nz), f32),
            vmem((planes, ny, nz), jnp.int32), vmem((planes, ny, nz), f32), vmem((2, planes, ny, nz), f32),
            vmem((2, 3 * planes) + plane, f32), vmem((3, planes) + plane, f32),
            vmem((comps, 3 * planes) + plane, f32), vmem((3 * planes,) + plane, f32),
            vmem((comps, 2, 9, modes, nz), f32), vmem(tiles_in, f32),
            vmem(tiles_out, f32), vmem(tiles_out, f32),
            vmem(tiles_in, f32), vmem(tiles_in, f32),
            vmem((comps, every, 8, nz), f32),
            vmem((every, 2 * every), f32), vmem((groups,) + tile, f32),
            vmem(tile, f32), vmem((side,) + tile, f32),
            vmem(tile, f32), vmem((side,) + tile, f32),
            vmem(tile, f32), vmem((groups,) + tile, f32),
            dma((comps + 2,)), dma((2,)), dma((2,)),
            dma((2, comps)), dma((2, comps)), dma((comps, 3)), dma((comps,)),
            dma((comps,)), dma((comps,)), dma((comps,)), dma((comps,)),
            dma((2 * comps,)), dma((comps,)), dma((4,)), dma((4,)),
        ],
        compiler_params=pltpu.CompilerParams(
            collective_id=0, has_side_effects=True, vmem_limit_bytes=48 * 1024 * 1024),
    )(pltpu.with_memory_space_constraint(start_modes, pltpu.HBM),
      pltpu.with_memory_space_constraint(materials, pltpu.HBM),
      pltpu.with_memory_space_constraint(stiffness_table, pltpu.HBM))


def solution(mesh):
    return jax.shard_map(
        functools.partial(shards, mesh.shape["blk"], mesh.shape["mode"]),
        mesh=mesh,
        in_specs=(P("mode", None, "blk", None, None), P("blk", None, None), P()),
        out_specs=(P("mode", None, "blk", None, None), P()),
        check_vma=False,
    )
```

time: 88.8 us -> 83.8 us (0.944)
  Pallas kernels: 85.3 us -> 81.5 us
  local copies, waits for them, and re-layouts: 2.71 us -> 1.5 us
    pallas_call x1, Pallas kernels: 85.3 us -> 81.5 us  [shards(): pl.pallas_call(functools.partial(kernel, blks, groups), out_shape=(jax.Sh...]
    unnamed x4 -> x2, local copies, waits for them, and re-layouts: 2.71 us -> 1.5 us
where the time goes in v3:
time: 83.8 us; the launch traced here: 83.6 us
  Pallas kernels  81.5 us (97%)
  local copies, waits for them, and re-layouts  1.5 us (2%)
    pallas_call x1, Pallas kernels, shards(): pl.pallas_call(functools.partial(kernel, blks, groups), out_shape=(jax.Sh...  81.5 us

profile of v3, /device:TPU:1, one launch (start us, length us, event | category | flops | bytes accessed | tf_op | source)
XLA Modules:
  0.0 83.6 jit_solution(15431411664809715608)
XLA Ops:
  0.6 81.5 %shard_map.50 = (f32[8,3,4,16,128]{4,3,2,1,0:T(8,128)S(1)}, f32[64,64]{1,0:T(8,128)S(1)}) custom-call(f32[8,3,4,16,128]{4,3,2,1,0:T(8,128)} %x_ref.1, s32[4,16,128]{2,1,0:T(8,128)} %mat_ref.1, f32[8]{0:T(128)} %tab_hbm.1), custom_call_target="tpu_custom_call" | custom-call | tf_op jit(solution)/shard_map/pallas_call | solution.py:467
  82.1 0.9 %copy.7 = f32[8,3,4,16,128]{4,3,2,1,0:T(8,128)} copy(f32[8,3,4,16,128]{4,3,2,1,0:T(8,128)S(1)} %get-tuple-element.4) | data formatting | bytes 1572864
  83.0 0.6 copy.8

commit v4 on v3

--- a/solution.py
+++ b/solution.py
@@ -18,11 +18,11 @@
 
 def kernel(blks, groups, x_ref, mat_ref, tab_hbm, out_ref, proj_ref,
            tab_ref, own, mats, table, table_in, coef, close, field, odd, edge_out, edge_in,
-           filt_out, image_out, filt_in, image_in,
+           filt_out, image_out, filt_in, image_in, again_in, again, inverse_ref,
            back, part, part_in, tile_y, in_y, tile_z, in_z, tile_all, total,
            load, table_send, table_recv, near_send, near_recv, edge_send, edge_recv,
            filt_send, filt_recv, image_send, image_recv,
-           back_send, back_recv, sum_send, sum_recv):
+           back_send, back_recv, own_send, again_send, again_recv, sum_send, sum_recv):
     modes, comps, planes, ny, nz = x_ref.shape
     every = modes * groups
     halves = ny // 8
@@ -46,6 +46,9 @@
 
     my_tile = tile_of(me)
 
+    def far_first(count):
+        return sorted(range(1, count), key=lambda step: abs(2 * step - count))
+
     def remote(src, dst, send, recv, to_blk, to_mode):
         return pltpu.make_async_remote_copy(
             src_ref=src, dst_ref=dst, send_sem=send, recv_sem=recv,
@@ -55,6 +58,17 @@
         pltpu.make_async_copy(ref, ref, semaphore).wait()
 
     owner_last, owner_first, owner_row = 3, 4, 0
+
+    load_mats = pltpu.make_async_copy(mat_ref, mats, load.at[comps])
+    load_mats.start()
+    load_tab = pltpu.make_async_copy(tab_hbm, tab_ref, load.at[comps + 1])
+    load_tab.start()
+
+    def load_own(comp):
+        return pltpu.make_async_copy(x_ref.at[:, comp], own.at[comp], load.at[comp])
+
+    for comp in range(comps):
+        load_own(comp).start()
 
     barrier = pltpu.get_barrier_semaphore()
 
@@ -79,17 +93,6 @@
         for mode in range(groups):
             greet(left, mode)
 
-    load_mats = pltpu.make_async_copy(mat_ref, mats, load.at[comps])
-    load_mats.start()
-    load_tab = pltpu.make_async_copy(tab_hbm, tab_ref, load.at[comps + 1])
-    load_tab.start()
-
-    def load_own(comp):
-        return pltpu.make_async_copy(x_ref.at[:, comp], own.at[comp], load.at[comp])
-
-    for comp in range(comps):
-        load_own(comp).start()
-
     def over(count, body, unroll=1):
         def run(at, carry):
             body(at)
@@ -134,7 +137,7 @@
         table[plane] = values
         close[0, plane] = all_modes(jnp.sqrt(values))
 
-    over(planes, own_root)
+    over(planes, own_root, planes)
 
     def weigh(comp):
         load_own(comp).wait()
@@ -143,7 +146,7 @@
         def body(plane):
             for y in range(ny):
                 field[comp, planes + plane, y] = close[0, plane, y] * rows[pl.ds(plane * ny + y, modes, stride=planes * ny)]
-        over(planes, body)
+        over(planes, body, 2)
 
     weigh(0)
     pl.semaphore_wait(barrier, 5 + (groups - 1) + 2 * (side - 1))
@@ -342,14 +345,27 @@
 
     over(comps, add_sums)
 
-    def exchange(phase, count, my_slot, source, target, own_tile, device):
-        for step in range(1, count):
+    opposite = mode_peer(groups // 2)
+    core = lax.rem(me, 2)
+    sibling = me + 1 - 2 * core
+
+    def spread_again():
+        def body(comp):
+            for step in far_first(groups):
+                peer = mode_peer(step)
+                remote(filt_out.at[comp, tile_of(mode_peer(step + groups // 2))], again_in.at[comp, :, my_modes()],
+                       again_send.at[comp], again_recv.at[comp], blk, peer).start()
+            again_in[comp, :, my_modes()] = filt_out[comp, tile_of(opposite)]
+        over(comps, body)
+
+    def exchange(phase, count, my_slot, source, target, own_tile, device, meanwhile=None):
+        for step in far_first(count):
             to_blk, to_mode, slot = device(step)
             remote(source(slot), target.at[my_slot], sum_send.at[phase], sum_recv.at[phase], to_blk, to_mode).start()
         target[my_slot] = own_tile
-        most = target.at[pl.ds(0, count - 1)]
-        arrived(most, sum_recv.at[phase])
-        arrived(most, sum_send.at[phase])
+        if meanwhile is not None:
+            meanwhile()
+        arrived(target.at[pl.ds(0, count - 1)], sum_recv.at[phase])
 
     def added(slots, count):
         result = slots[0]
@@ -358,7 +374,7 @@
         return result
 
     exchange(0, groups, me, lambda slot: part.at[pl.ds(pl.multiple_of(slot * 8, 8), 8)], part_in,
-             part[pl.ds(pl.multiple_of(me * 8, 8), 8)], lambda step: (blk, mode_peer(step), mode_peer(step)))
+             part[pl.ds(pl.multiple_of(me * 8, 8), 8)], lambda step: (blk, mode_peer(step), mode_peer(step)), spread_again)
     tile = added(part_in, groups)
     tile_y[...] = tile
     exchange(1, side, my_y, lambda slot: tile_y, in_y, tile, lambda step: (y_peer(step), me, 0))
@@ -403,31 +419,59 @@
     work = jnp.concatenate(blocks, axis=0)
     diagonal = jnp.sum(jnp.where(lane_at == row_at + every, work, 0.0), axis=1, keepdims=True)
     inverse = (work / jnp.sqrt(diagonal))[:, :every]
-
-    def place():
-        return lax.div(my_tile, halves), pl.ds(pl.multiple_of(lax.rem(my_tile, halves) * 8, 8), 8)
+    inverse_ref[...] = inverse
+
+    def place(tile):
+        return lax.div(tile, halves), pl.ds(pl.multiple_of(lax.rem(tile, halves) * 8, 8), 8)
 
     def back_copies(comp):
-        plane, rows = place()
-        return [remote(back.at[comp, pl.ds(mode_peer(step) * modes, modes)], out_ref.at[:, comp, plane, rows],
-                       back_send.at[comp], back_recv.at[comp], blk, mode_peer(step)) for step in range(1, groups)]
-
-    def own_copy(comp):
-        plane, rows = place()
-        return pltpu.make_async_copy(back.at[comp, pl.ds(me * modes, modes)], out_ref.at[:, comp, plane, rows],
-                                     back_send.at[comps + comp])
+        plane, rows = place(my_tile)
+        copies = []
+        for step in far_first(groups):
+            peer = mode_peer(step)
+            copies.append((peer, remote(back.at[comp, pl.ds(peer * modes, modes)], out_ref.at[:, comp, plane, rows],
+                                        back_send.at[comp], back_recv.at[comp], blk, peer)))
+        return copies
+
+    def own_copies(comp):
+        plane, rows = place(my_tile)
+        other_plane, other_rows = place(tile_of(opposite))
+        return (pltpu.make_async_copy(back.at[comp, pl.ds(me * modes, modes)], out_ref.at[:, comp, plane, rows],
+                                      own_send.at[0, comp]),
+                pltpu.make_async_copy(again.at[comp, pl.ds(core * modes, modes)], out_ref.at[:, comp, other_plane, other_rows],
+                                      own_send.at[1, comp]))
+
+    def sibling_copy(comp):
+        plane, rows = place(tile_of(opposite))
+        return remote(again.at[comp, pl.ds((1 - core) * modes, modes)], out_ref.at[:, comp, plane, rows],
+                      back_send.at[comp], back_recv.at[comp], blk, sibling)
 
     def give_back(comp):
         filt = jnp.concatenate([filt_in[comp, row] for row in range(8)], axis=1)
         result = jnp.dot(inverse, filt, precision=HIGH, preferred_element_type=jnp.float32)
         for row in range(8):
             back[comp, :, row] = result[:, row * nz:(row + 1) * nz]
-        for copy in back_copies(comp):
-            copy.start()
-        own_copy(comp).start()
+        for peer, copy in back_copies(comp):
+            @pl.when(lax.div(peer, 2) != lax.div(opposite, 2))
+            def _():
+                copy.start()
+        own_copies(comp)[0].start()
+
+    def give_sibling(comp):
+        arrived(again_in.at[comp, :, pl.ds(0, (groups - 1) * modes)], again_recv.at[comp])
+        arrived(again_in.at[comp, :, pl.ds(0, (groups - 1) * modes)], again_send.at[comp])
+        filt = jnp.concatenate([again_in[comp, row] for row in range(8)], axis=1)
+        mine = inverse_ref[pl.ds(pl.multiple_of((me - core) * modes, 2 * modes), 2 * modes), :]
+        result = jnp.dot(mine, filt, precision=HIGH, preferred_element_type=jnp.float32)
+        for row in range(8):
+            again[comp, :, row] = result[:, row * nz:(row + 1) * nz]
+        sibling_copy(comp).start()
+        own_copies(comp)[1].start()
 
     for comp in range(comps):
         give_back(comp)
+    for comp in range(comps):
+        give_sibling(comp)
     half = jnp.dot(inverse, cross, precision=HIGH, preferred_element_type=jnp.float32)
     product = lax.dot_general(half, inverse, (((1,), (1,)), ((), ())), precision=HIGH,
                               preferred_element_type=jnp.float32)
@@ -446,12 +490,15 @@
             for copy in to_right:
                 copy.wait_send()
 
-        own_copy(comp).wait()
-        most = back.at[comp, pl.ds(0, (groups - 1) * modes)]
+        for copy in own_copies(comp):
+            copy.wait()
+        most = back.at[comp, pl.ds(0, (groups - 2) * modes)]
         arrived(most, back_recv.at[comp])
         arrived(most, back_send.at[comp])
 
     over(comps, finish)
+    for phase, target, count in ((0, part_in, groups), (1, in_y, side), (2, in_z, side), (3, total, groups)):
+        arrived(target.at[pl.ds(0, count - 1)], sum_send.at[phase])
 
 
 def shards(blks, groups, start_modes, materials, stiffness_table):
@@ -479,6 +526,7 @@
             vmem((comps, 2, 9, modes, nz), f32), vmem(tiles_in, f32),
             vmem(tiles_out, f32), vmem(tiles_out, f32),
             vmem(tiles_in, f32), vmem(tiles_in, f32),
+            vmem(tiles_in, f32), vmem((comps, 2 * modes, 8, nz), f32), vmem((every, every), f32),
             vmem((comps, every, 8, nz), f32),
             vmem((every, 2 * every), f32), vmem((groups,) + tile, f32),
             vmem(tile, f32), vmem((side,) + tile, f32),
@@ -487,7 +535,7 @@
             dma((comps + 2,)), dma((2,)), dma((2,)),
             dma((2, comps)), dma((2, comps)), dma((comps, 3)), dma((comps,)),
             dma((comps,)), dma((comps,)), dma((comps,)), dma((comps,)),
-            dma((2 * comps,)), dma((comps,)), dma((4,)), dma((4,)),
+            dma((comps,)), dma((comps,)), dma((2, comps)), dma((comps,)), dma((comps,)), dma((4,)), dma((4,)),
         ],
         compiler_params=pltpu.CompilerParams(
             collective_id=0, has_side_effects=True, vmem_limit_bytes=48 * 1024 * 1024),

time: 83.8 us -> 78.9 us (0.942)
  Pallas kernels: 81.5 us -> 76.7 us
    pallas_call x1, Pallas kernels: 81.5 us -> 76.7 us  [shards(): pl.pallas_call(functools.partial(kernel, blks, groups), out_shape=(jax.Sh...]
where the time goes in v4:
time: 78.9 us; the launch traced here: 78.8 us
  Pallas kernels  76.7 us (97%)
  local copies, waits for them, and re-layouts  1.5 us (2%)
    pallas_call x1, Pallas kernels, shards(): pl.pallas_call(functools.partial(kernel, blks, groups), out_shape=(jax.Sh...  76.7 us

profile of v4, /device:TPU:1, one launch (start us, length us, event | category | flops | bytes accessed | tf_op | source)
XLA Modules:
  0.0 78.8 jit_solution(14217269219625924992)
XLA Ops:
  0.6 76.7 %shard_map.50 = (f32[8,3,4,16,128]{4,3,2,1,0:T(8,128)S(1)}, f32[64,64]{1,0:T(8,128)S(1)}) custom-call(f32[8,3,4,16,128]{4,3,2,1,0:T(8,128)} %x_ref.1, s32[4,16,128]{2,1,0:T(8,128)} %mat_ref.1, f32[8]{0:T(128)} %tab_hbm.1), custom_call_target="tpu_custom_call" | custom-call | tf_op jit(solution)/shard_map/pallas_call | solution.py:514
  77.3 0.9 %copy.7 = f32[8,3,4,16,128]{4,3,2,1,0:T(8,128)} copy(f32[8,3,4,16,128]{4,3,2,1,0:T(8,128)S(1)} %get-tuple-element.4) | data formatting | bytes 1572864
  78.2 0.6 copy.8

commit v5 on v4

--- a/solution.py
+++ b/solution.py
@@ -19,7 +19,7 @@
 def kernel(blks, groups, x_ref, mat_ref, tab_hbm, out_ref, proj_ref,
            tab_ref, own, mats, table, table_in, coef, close, field, odd, edge_out, edge_in,
            filt_out, image_out, filt_in, image_in, again_in, again, inverse_ref,
-           back, part, part_in, tile_y, in_y, tile_z, in_z, tile_all, total,
+           back, part, part_in, in_y, in_z, total, tiles_sent,
            load, table_send, table_recv, near_send, near_recv, edge_send, edge_recv,
            filt_send, filt_recv, image_send, image_recv,
            back_send, back_recv, own_send, again_send, again_recv, sum_send, sum_recv):
@@ -146,7 +146,7 @@
         def body(plane):
             for y in range(ny):
                 field[comp, planes + plane, y] = close[0, plane, y] * rows[pl.ds(plane * ny + y, modes, stride=planes * ny)]
-        over(planes, body, 2)
+        over(planes, body, 4)
 
     weigh(0)
     pl.semaphore_wait(barrier, 5 + (groups - 1) + 2 * (side - 1))
@@ -178,16 +178,19 @@
         table_copy(0).start()
         near_copy(0, 0).start()
 
-    for comp in range(1, comps):
+    def start_near(comp):
+        @pl.when(jnp.logical_not(no_left))
+        def _():
+            near_copy(comp, 1).start()
+
+        @pl.when(jnp.logical_not(no_right))
+        def _():
+            near_copy(comp, 0).start()
+
+    weigh(1)
+    start_near(1)
+    for comp in range(2, comps):
         weigh(comp)
-
-        @pl.when(jnp.logical_not(no_left))
-        def _():
-            near_copy(comp, 1).start()
-
-        @pl.when(jnp.logical_not(no_right))
-        def _():
-            near_copy(comp, 0).start()
 
     def own_coefficients(plane):
         values = table[plane]
@@ -240,7 +243,7 @@
             else:
                 new = new - other[plane]
             other[plane] = new
-        over(3 * planes - 2 * first, body, 2)
+        over(3 * planes - 2 * first, body, 3 * planes - 2 * first)
 
     def finals(comp):
         first, last = field[comp, planes, :9], field[comp, 2 * planes - 1, 8:]
@@ -270,7 +273,7 @@
             for half in range(halves):
                 filt_out[comp, plane * halves + half] = filt[8 * half:8 * half + 8]
                 image_out[comp, plane * halves + half] = image[8 * half:8 * half + 8]
-        over(planes, body, 2)
+        over(planes, body, 4)
 
     def my_modes():
         return pl.ds(pl.multiple_of(me * modes, modes), modes)
@@ -301,7 +304,15 @@
             advance(step, comp)
         finals(comp)
         spread(filt_out, filt_in, filt_send, filt_recv, comp)
-        spread(image_out, image_in, image_send, image_recv, comp)
+
+        @pl.when(comp + 1 < comps)
+        def _():
+            spread(image_out, image_in, image_send, image_recv, comp)
+
+        @pl.when(comp + 2 < comps)
+        def _():
+            start_near(comp + 2)
+
         filt_in[comp, :, my_modes()] = filt_out[comp, my_tile]
         image_in[comp, :, my_modes()] = image_out[comp, my_tile]
 
@@ -329,66 +340,94 @@
                 at = pl.ds(group * modes, modes)
                 image_in[comp, 7, at] = image_in[comp, 7, at] - (2.0 * close[0, 0, 7]) * edge_in[comp, 0, at]
 
+    def products(left, right):
+        return lax.dot_general(left, right, (((1,), (1,)), ((), ())), precision=HIGH, preferred_element_type=jnp.float32)
+
+    def pairs(ref, comp, first):
+        return jnp.concatenate([ref[comp, first], ref[comp, first + 1]], axis=1)
+
     part[...] = jnp.zeros_like(part)
 
-    def add_sums(comp):
+    def add_gram(comp):
         spread_wait(filt_in, filt_send, filt_recv, comp)
+        sums = part[0]
+        for row in range(0, 8, 2):
+            filt = pairs(filt_in, comp, row)
+            sums = sums + products(filt, jnp.concatenate([filt, filt], axis=0))
+        part[0] = sums
+
+    def add_cross(comp):
         spread_wait(image_in, image_send, image_recv, comp)
         add_edges(comp)
-        sums = part[...]
+        sums = part[1, :, :every]
         for row in range(0, 8, 2):
-            filt = jnp.concatenate([filt_in[comp, row], filt_in[comp, row + 1]], axis=1)
-            image = jnp.concatenate([image_in[comp, row], image_in[comp, row + 1]], axis=1)
-            sums = sums + lax.dot_general(filt, jnp.concatenate([image, filt], axis=0), (((1,), (1,)), ((), ())),
-                                          precision=HIGH, preferred_element_type=jnp.float32)
-        part[...] = sums
-
-    over(comps, add_sums)
+            sums = sums + products(pairs(filt_in, comp, row), pairs(image_in, comp, row))
+        part[1, :, :every] = sums
+
+    over(comps, add_gram)
 
     opposite = mode_peer(groups // 2)
     core = lax.rem(me, 2)
     sibling = me + 1 - 2 * core
 
-    def spread_again():
-        def body(comp):
-            for step in far_first(groups):
-                peer = mode_peer(step)
-                remote(filt_out.at[comp, tile_of(mode_peer(step + groups // 2))], again_in.at[comp, :, my_modes()],
-                       again_send.at[comp], again_recv.at[comp], blk, peer).start()
-            again_in[comp, :, my_modes()] = filt_out[comp, tile_of(opposite)]
-        over(comps, body)
-
-    def exchange(phase, count, my_slot, source, target, own_tile, device, meanwhile=None):
+    def spread_again(comp):
+        for step in far_first(groups):
+            peer = mode_peer(step)
+            remote(filt_out.at[comp, tile_of(mode_peer(step + groups // 2))], again_in.at[comp, :, my_modes()],
+                   again_send.at[comp], again_recv.at[comp], blk, peer).start()
+        again_in[comp, :, my_modes()] = filt_out[comp, tile_of(opposite)]
+
+    def slots_of(which, phase):
+        return ((part_in, groups, me), (in_y, side, my_y), (in_z, side, my_z), (total, groups, me))[phase]
+
+    def send_sums(which, phase):
+        target, count, my_slot = slots_of(which, phase)
+        if phase == 0:
+            own_tile = part[which, pl.ds(pl.multiple_of(me * 8, 8), 8)]
+        else:
+            before, before_count, _ = slots_of(which, phase - 1)
+            own_tile = before[which, 0]
+            for slot in range(1, before_count):
+                own_tile = own_tile + before[which, slot]
+            tiles_sent[which, phase - 1] = own_tile
         for step in far_first(count):
-            to_blk, to_mode, slot = device(step)
-            remote(source(slot), target.at[my_slot], sum_send.at[phase], sum_recv.at[phase], to_blk, to_mode).start()
-        target[my_slot] = own_tile
-        if meanwhile is not None:
-            meanwhile()
-        arrived(target.at[pl.ds(0, count - 1)], sum_recv.at[phase])
-
-    def added(slots, count):
-        result = slots[0]
-        for slot in range(1, count):
-            result = result + slots[slot]
-        return result
-
-    exchange(0, groups, me, lambda slot: part.at[pl.ds(pl.multiple_of(slot * 8, 8), 8)], part_in,
-             part[pl.ds(pl.multiple_of(me * 8, 8), 8)], lambda step: (blk, mode_peer(step), mode_peer(step)), spread_again)
-    tile = added(part_in, groups)
-    tile_y[...] = tile
-    exchange(1, side, my_y, lambda slot: tile_y, in_y, tile, lambda step: (y_peer(step), me, 0))
-    tile = added(in_y, side)
-    tile_z[...] = tile
-    exchange(2, side, my_z, lambda slot: tile_z, in_z, tile, lambda step: (z_peer(step), me, 0))
-    tile = added(in_z, side)
-    tile_all[...] = tile
-    exchange(3, groups, me, lambda slot: tile_all, total, tile, lambda step: (blk, mode_peer(step), 0))
-
-    sums = total[...].reshape((every, 2 * every))
+            if phase == 0 or phase == 3:
+                to_blk, to_mode = blk, mode_peer(step)
+            else:
+                to_blk, to_mode = (y_peer, z_peer)[phase - 1](step), me
+            if phase == 0:
+                source = part.at[which, pl.ds(pl.multiple_of(mode_peer(step) * 8, 8), 8)]
+            else:
+                source = tiles_sent.at[which, phase - 1]
+            remote(source, target.at[which, my_slot], sum_send.at[which, phase], sum_recv.at[which, phase],
+                   to_blk, to_mode).start()
+        target[which, my_slot] = own_tile
+
+    def wait_sums(which, phase):
+        target, count, _ = slots_of(which, phase)
+        arrived(target.at[which, pl.ds(0, count - 1)], sum_recv.at[which, phase])
+
+    send_sums(0, 0)
+    spread(image_out, image_in, image_send, image_recv, comps - 1)
+    over(comps - 1, spread_again)
+    wait_sums(0, 0)
+    send_sums(0, 1)
+    over(comps, add_cross)
+    send_sums(1, 0)
+    spread_again(comps - 1)
+    wait_sums(0, 1)
+    send_sums(0, 2)
+    wait_sums(1, 0)
+    send_sums(1, 1)
+    wait_sums(0, 2)
+    send_sums(0, 3)
+    wait_sums(1, 1)
+    send_sums(1, 2)
+    wait_sums(0, 3)
+
+    sums = total[0].reshape((every, 2 * every))
     row_at = lax.broadcasted_iota(jnp.int32, (every, 2 * every), 0)
     lane_at = lax.broadcasted_iota(jnp.int32, (every, 2 * every), 1)
-    cross = sums[:, :every]
     work = jnp.where(lane_at < every, jnp.where(lane_at == row_at, 1.0, 0.0), sums)
     blocks = [work[8 * j:8 * j + 8] for j in range(every // 8)]
     sub = lax.broadcasted_iota(jnp.int32, (8, 2 * every), 0)
@@ -468,10 +507,15 @@
         sibling_copy(comp).start()
         own_copies(comp)[1].start()
 
-    for comp in range(comps):
+    give_back(0)
+    wait_sums(1, 2)
+    send_sums(1, 3)
+    for comp in range(1, comps):
         give_back(comp)
     for comp in range(comps):
         give_sibling(comp)
+    wait_sums(1, 3)
+    cross = total[1].reshape((every, 2 * every))[:, :every]
     half = jnp.dot(inverse, cross, precision=HIGH, preferred_element_type=jnp.float32)
     product = lax.dot_general(half, inverse, (((1,), (1,)), ((), ())), precision=HIGH,
                               preferred_element_type=jnp.float32)
@@ -497,8 +541,10 @@
         arrived(most, back_send.at[comp])
 
     over(comps, finish)
-    for phase, target, count in ((0, part_in, groups), (1, in_y, side), (2, in_z, side), (3, total, groups)):
-        arrived(target.at[pl.ds(0, count - 1)], sum_send.at[phase])
+    for which in range(2):
+        for phase in range(4):
+            target, count, _ = slots_of(which, phase)
+            arrived(target.at[which, pl.ds(0, count - 1)], sum_send.at[which, phase])
 
 
 def shards(blks, groups, start_modes, materials, stiffness_table):
@@ -528,14 +574,12 @@
             vmem(tiles_in, f32), vmem(tiles_in, f32),
             vmem(tiles_in, f32), vmem((comps, 2 * modes, 8, nz), f32), vmem((every, every), f32),
             vmem((comps, every, 8, nz), f32),
-            vmem((every, 2 * every), f32), vmem((groups,) + tile, f32),
-            vmem(tile, f32), vmem((side,) + tile, f32),
-            vmem(tile, f32), vmem((side,) + tile, f32),
-            vmem(tile, f32), vmem((groups,) + tile, f32),
+            vmem((2, every, 2 * every), f32), vmem((2, groups) + tile, f32), vmem((2, side) + tile, f32),
+            vmem((2, side) + tile, f32), vmem((2, groups) + tile, f32), vmem((2, 3) + tile, f32),
             dma((comps + 2,)), dma((2,)), dma((2,)),
             dma((2, comps)), dma((2, comps)), dma((comps, 3)), dma((comps,)),
             dma((comps,)), dma((comps,)), dma((comps,)), dma((comps,)),
-            dma((comps,)), dma((comps,)), dma((2, comps)), dma((comps,)), dma((comps,)), dma((4,)), dma((4,)),
+            dma((comps,)), dma((comps,)), dma((2, comps)), dma((comps,)), dma((comps,)), dma((2, 4)), dma((2, 4)),
         ],
         compiler_params=pltpu.CompilerParams(
             collective_id=0, has_side_effects=True, vmem_limit_bytes=48 * 1024 * 1024),

time: 78.9 us -> 75.4 us (0.956)
  Pallas kernels: 76.7 us -> 73.2 us
    pallas_call x1, Pallas kernels: 76.7 us -> 73.2 us  [shards(): pl.pallas_call(functools.partial(kernel, blks, groups), out_shape=(jax.Sh...]
where the time goes in v5:
time: 75.4 us; the launch traced here: 75.3 us
  Pallas kernels  73.2 us (97%)
  local copies, waits for them, and re-layouts  1.5 us (2%)
    pallas_call x1, Pallas kernels, shards(): pl.pallas_call(functools.partial(kernel, blks, groups), out_shape=(jax.Sh...  73.2 us

profile of v5, /device:TPU:1, one launch (start us, length us, event | category | flops | bytes accessed | tf_op | source)
XLA Modules:
  0.0 75.3 jit_solution(7875511456565338796)
XLA Ops:
  0.6 73.2 %shard_map.50 = (f32[8,3,4,16,128]{4,3,2,1,0:T(8,128)S(1)}, f32[64,64]{1,0:T(8,128)S(1)}) custom-call(f32[8,3,4,16,128]{4,3,2,1,0:T(8,128)} %x_ref.1, s32[4,16,128]{2,1,0:T(8,128)} %mat_ref.1, f32[8]{0:T(128)} %tab_hbm.1), custom_call_target="tpu_custom_call" | custom-call | tf_op jit(solution)/shard_map/pallas_call | solution.py:560
  73.8 0.9 %copy.7 = f32[8,3,4,16,128]{4,3,2,1,0:T(8,128)} copy(f32[8,3,4,16,128]{4,3,2,1,0:T(8,128)S(1)} %get-tuple-element.4) | data formatting | bytes 1572864
  74.7 0.6 copy.8

commit v6 on v5

--- a/solution.py
+++ b/solution.py
@@ -20,9 +20,10 @@
            tab_ref, own, mats, table, table_in, coef, close, field, odd, edge_out, edge_in,
            filt_out, image_out, filt_in, image_in, again_in, again, inverse_ref,
            back, part, part_in, in_y, in_z, total, tiles_sent,
+           gram_part, gram_out, gram_in, plane_in, gram_total, gram_tiles,
            load, table_send, table_recv, near_send, near_recv, edge_send, edge_recv,
            filt_send, filt_recv, image_send, image_recv,
-           back_send, back_recv, own_send, again_send, again_recv, sum_send, sum_recv):
+           back_send, back_recv, own_send, again_send, again_recv, sum_send, sum_recv, gram_send, gram_recv):
     modes, comps, planes, ny, nz = x_ref.shape
     every = modes * groups
     halves = ny // 8
@@ -75,11 +76,14 @@
     def greet(to_blk, to_mode):
         pl.semaphore_signal(barrier, inc=1, device_id={"blk": to_blk, "mode": to_mode}, device_id_type=MESH)
 
-    greet(left, me)
-    greet(right, me)
-    for step in range(1, side):
-        greet(y_peer(step), me)
-        greet(z_peer(step), me)
+    around = sorted(((dz, dy) for dz in range(side) for dy in range(side) if dz or dy),
+                    key=lambda at: -sum(min(d, side - d) for d in at))
+
+    def plane_peer(dz, dy):
+        return lax.rem(my_z + dz, side) * side + lax.rem(my_y + dy, side)
+
+    for dz, dy in around:
+        greet(plane_peer(dz, dy), me)
     for step in range(1, groups):
         greet(blk, mode_peer(step))
 
@@ -149,7 +153,7 @@
         over(planes, body, 4)
 
     weigh(0)
-    pl.semaphore_wait(barrier, 5 + (groups - 1) + 2 * (side - 1))
+    pl.semaphore_wait(barrier, 3 + (groups - 1) + (blks - 1))
 
     def table_copy(slot):
         return remote(table, table_in.at[slot], table_send.at[slot], table_recv.at[slot], (right, left)[slot], me)
@@ -245,7 +249,30 @@
             other[plane] = new
         over(3 * planes - 2 * first, body, 3 * planes - 2 * first)
 
-    def finals(comp):
+    def my_modes():
+        return pl.ds(pl.multiple_of(me * modes, modes), modes)
+
+    def spread(source, target, send, recv, comp):
+        for step in range(1, groups):
+            peer = mode_peer(step)
+            remote(source.at[comp, tile_of(peer)], target.at[comp, :, my_modes()],
+                   send.at[comp], recv.at[comp], blk, peer).start()
+
+    def spread_wait(target, send, recv, comp):
+        most = target.at[comp, :, pl.ds(0, (groups - 1) * modes)]
+        arrived(most, recv.at[comp])
+        arrived(most, send.at[comp])
+
+    def put(target, comp, plane, value):
+        for half in range(halves):
+            target[comp, plane * halves + half] = value[8 * half:8 * half + 8]
+
+    def final_filter(comp):
+        def body(plane):
+            put(filt_out, comp, plane, field[comp, planes + plane] * close[1, plane])
+        over(planes, body, planes)
+
+    def final_image(comp):
         first, last = field[comp, planes, :9], field[comp, 2 * planes - 1, 8:]
         edge_out[comp, 1, :8] = box_z(first[:8] + (first[1:] + jnp.concatenate([none, first[:7]], axis=0)))
         edge_out[comp, 0] = box_z(jnp.concatenate([none, last], axis=0) + (
@@ -268,26 +295,9 @@
         def body(plane):
             at = planes + plane
             w = field[comp, at]
-            filt = w * close[1, plane]
-            image = close[2, plane] * w - close[0, plane] * box(field[comp, at - 1] + w + field[comp, at + 1])
-            for half in range(halves):
-                filt_out[comp, plane * halves + half] = filt[8 * half:8 * half + 8]
-                image_out[comp, plane * halves + half] = image[8 * half:8 * half + 8]
+            put(image_out, comp, plane,
+                close[2, plane] * w - close[0, plane] * box(field[comp, at - 1] + w + field[comp, at + 1]))
         over(planes, body, 4)
-
-    def my_modes():
-        return pl.ds(pl.multiple_of(me * modes, modes), modes)
-
-    def spread(source, target, send, recv, comp):
-        for step in range(1, groups):
-            peer = mode_peer(step)
-            remote(source.at[comp, tile_of(peer)], target.at[comp, :, my_modes()],
-                   send.at[comp], recv.at[comp], blk, peer).start()
-
-    def spread_wait(target, send, recv, comp):
-        most = target.at[comp, :, pl.ds(0, (groups - 1) * modes)]
-        arrived(most, recv.at[comp])
-        arrived(most, send.at[comp])
 
     def filter_one(comp):
         @pl.when(jnp.logical_not(no_left))
@@ -302,17 +312,18 @@
 
         for step in range(DEGREE):
             advance(step, comp)
-        finals(comp)
+        final_filter(comp)
         spread(filt_out, filt_in, filt_send, filt_recv, comp)
 
-        @pl.when(comp + 1 < comps)
-        def _():
-            spread(image_out, image_in, image_send, image_recv, comp)
+        @pl.when(comp > 0)
+        def _():
+            spread(image_out, image_in, image_send, image_recv, comp - 1)
 
         @pl.when(comp + 2 < comps)
         def _():
             start_near(comp + 2)
 
+        final_image(comp)
         filt_in[comp, :, my_modes()] = filt_out[comp, my_tile]
         image_in[comp, :, my_modes()] = image_out[comp, my_tile]
 
@@ -347,22 +358,23 @@
         return jnp.concatenate([ref[comp, first], ref[comp, first + 1]], axis=1)
 
     part[...] = jnp.zeros_like(part)
+    gram_part[...] = jnp.zeros_like(gram_part)
 
     def add_gram(comp):
         spread_wait(filt_in, filt_send, filt_recv, comp)
-        sums = part[0]
+        sums = gram_part[...]
         for row in range(0, 8, 2):
             filt = pairs(filt_in, comp, row)
-            sums = sums + products(filt, jnp.concatenate([filt, filt], axis=0))
-        part[0] = sums
+            sums = sums + products(filt, filt)
+        gram_part[...] = sums
 
     def add_cross(comp):
         spread_wait(image_in, image_send, image_recv, comp)
         add_edges(comp)
-        sums = part[1, :, :every]
+        sums = part[:, :every]
         for row in range(0, 8, 2):
             sums = sums + products(pairs(filt_in, comp, row), pairs(image_in, comp, row))
-        part[1, :, :every] = sums
+        part[:, :every] = sums
 
     over(comps, add_gram)
 
@@ -377,58 +389,93 @@
                    again_send.at[comp], again_recv.at[comp], blk, peer).start()
         again_in[comp, :, my_modes()] = filt_out[comp, tile_of(opposite)]
 
-    def slots_of(which, phase):
+    low = pl.ds(0, 4)
+
+    def pack_gram():
+        sums = gram_part[...]
+        packed = jnp.concatenate([sums[:every // 2], sums[every // 2:]], axis=1)
+        for group in range(groups):
+            gram_out[group, :4] = packed[4 * group:4 * group + 4]
+
+    def send_gram_scatter():
+        for step in far_first(groups):
+            remote(gram_out.at[mode_peer(step), low], gram_in.at[me, low], gram_send.at[0], gram_recv.at[0],
+                   blk, mode_peer(step)).start()
+        gram_in[me, :4] = gram_out[me, :4]
+
+    def send_gram_plane():
+        tile = gram_in[0, :4]
+        for group in range(1, groups):
+            tile = tile + gram_in[group, :4]
+        gram_tiles[0, :4] = tile
+        for dz, dy in around:
+            remote(gram_tiles.at[0, low], plane_in.at[blk, low], gram_send.at[1], gram_recv.at[1],
+                   plane_peer(dz, dy), me).start()
+        plane_in[blk, :4] = tile
+
+    def send_gram_gather():
+        tiles = [plane_in[slot, :4] for slot in range(blks)]
+        while len(tiles) > 1:
+            tiles = [tiles[at] + tiles[at + 1] for at in range(0, len(tiles), 2)]
+        gram_tiles[1, :4] = tiles[0]
+        for step in far_first(groups):
+            remote(gram_tiles.at[1, low], gram_total.at[me, low], gram_send.at[2], gram_recv.at[2],
+                   blk, mode_peer(step)).start()
+        gram_total[me, :4] = tiles[0]
+
+    def wait_gram(phase, semaphores):
+        target, count = ((gram_in, groups), (plane_in, blks), (gram_total, groups))[phase]
+        arrived(target.at[pl.ds(0, count - 1), low], semaphores.at[phase])
+
+    def slots_of(phase):
         return ((part_in, groups, me), (in_y, side, my_y), (in_z, side, my_z), (total, groups, me))[phase]
 
-    def send_sums(which, phase):
-        target, count, my_slot = slots_of(which, phase)
+    def send_sums(phase):
+        target, count, my_slot = slots_of(phase)
         if phase == 0:
-            own_tile = part[which, pl.ds(pl.multiple_of(me * 8, 8), 8)]
+            own_tile = part[pl.ds(pl.multiple_of(me * 8, 8), 8)]
         else:
-            before, before_count, _ = slots_of(which, phase - 1)
-            own_tile = before[which, 0]
+            before, before_count, _ = slots_of(phase - 1)
+            own_tile = before[0]
             for slot in range(1, before_count):
-                own_tile = own_tile + before[which, slot]
-            tiles_sent[which, phase - 1] = own_tile
+                own_tile = own_tile + before[slot]
+            tiles_sent[phase - 1] = own_tile
         for step in far_first(count):
             if phase == 0 or phase == 3:
                 to_blk, to_mode = blk, mode_peer(step)
             else:
                 to_blk, to_mode = (y_peer, z_peer)[phase - 1](step), me
             if phase == 0:
-                source = part.at[which, pl.ds(pl.multiple_of(mode_peer(step) * 8, 8), 8)]
+                source = part.at[pl.ds(pl.multiple_of(mode_peer(step) * 8, 8), 8)]
             else:
-                source = tiles_sent.at[which, phase - 1]
-            remote(source, target.at[which, my_slot], sum_send.at[which, phase], sum_recv.at[which, phase],
-                   to_blk, to_mode).start()
-        target[which, my_slot] = own_tile
-
-    def wait_sums(which, phase):
-        target, count, _ = slots_of(which, phase)
-        arrived(target.at[which, pl.ds(0, count - 1)], sum_recv.at[which, phase])
-
-    send_sums(0, 0)
+                source = tiles_sent.at[phase - 1]
+            remote(source, target.at[my_slot], sum_send.at[phase], sum_recv.at[phase], to_blk, to_mode).start()
+        target[my_slot] = own_tile
+
+    def wait_sums(phase):
+        target, count, _ = slots_of(phase)
+        arrived(target.at[pl.ds(0, count - 1)], sum_recv.at[phase])
+
+    pack_gram()
+    send_gram_scatter()
     spread(image_out, image_in, image_send, image_recv, comps - 1)
     over(comps - 1, spread_again)
-    wait_sums(0, 0)
-    send_sums(0, 1)
+    wait_gram(0, gram_recv)
+    send_gram_plane()
     over(comps, add_cross)
-    send_sums(1, 0)
+    send_sums(0)
     spread_again(comps - 1)
-    wait_sums(0, 1)
-    send_sums(0, 2)
-    wait_sums(1, 0)
-    send_sums(1, 1)
-    wait_sums(0, 2)
-    send_sums(0, 3)
-    wait_sums(1, 1)
-    send_sums(1, 2)
-    wait_sums(0, 3)
-
-    sums = total[0].reshape((every, 2 * every))
+    wait_gram(1, gram_recv)
+    send_gram_gather()
+    wait_sums(0)
+    send_sums(1)
+    wait_gram(2, gram_recv)
+
+    packed = jnp.concatenate([gram_total[group, :4] for group in range(groups)], axis=0)
+    gram = jnp.concatenate([packed[:, :every], packed[:, every:]], axis=0)
     row_at = lax.broadcasted_iota(jnp.int32, (every, 2 * every), 0)
     lane_at = lax.broadcasted_iota(jnp.int32, (every, 2 * every), 1)
-    work = jnp.where(lane_at < every, jnp.where(lane_at == row_at, 1.0, 0.0), sums)
+    work = jnp.concatenate([jnp.where(lane_at == row_at, 1.0, 0.0)[:, :every], gram], axis=1)
     blocks = [work[8 * j:8 * j + 8] for j in range(every // 8)]
     sub = lax.broadcasted_iota(jnp.int32, (8, 2 * every), 0)
 
@@ -439,6 +486,9 @@
         return jnp.broadcast_to(block[row:row + 1], (8, 2 * every))
 
     for k in range(0, every, 2):
+        if k == every // 2:
+            wait_sums(1)
+            send_sums(2)
         j, r = divmod(k, 8)
         ones = [column(block, every + k) for block in blocks[j:]]
         twos = [column(block, every + k + 1) for block in blocks[j:]]
@@ -507,15 +557,14 @@
         sibling_copy(comp).start()
         own_copies(comp)[1].start()
 
-    give_back(0)
-    wait_sums(1, 2)
-    send_sums(1, 3)
-    for comp in range(1, comps):
+    for comp in range(comps):
         give_back(comp)
+    wait_sums(2)
+    send_sums(3)
     for comp in range(comps):
         give_sibling(comp)
-    wait_sums(1, 3)
-    cross = total[1].reshape((every, 2 * every))[:, :every]
+    wait_sums(3)
+    cross = total[...].reshape((every, 2 * every))[:, :every]
     half = jnp.dot(inverse, cross, precision=HIGH, preferred_element_type=jnp.float32)
     product = lax.dot_general(half, inverse, (((1,), (1,)), ((), ())), precision=HIGH,
                               preferred_element_type=jnp.float32)
@@ -541,10 +590,11 @@
         arrived(most, back_send.at[comp])
 
     over(comps, finish)
-    for which in range(2):
-        for phase in range(4):
-            target, count, _ = slots_of(which, phase)
-            arrived(target.at[which, pl.ds(0, count - 1)], sum_send.at[which, phase])
+    for phase in range(3):
+        wait_gram(phase, gram_send)
+    for phase in range(4):
+        target, count, _ = slots_of(phase)
+        arrived(target.at[pl.ds(0, count - 1)], sum_send.at[phase])
 
 
 def shards(blks, groups, start_modes, materials, stiffness_table):
@@ -574,12 +624,14 @@
             vmem(tiles_in, f32), vmem(tiles_in, f32),
             vmem(tiles_in, f32), vmem((comps, 2 * modes, 8, nz), f32), vmem((every, every), f32),
             vmem((comps, every, 8, nz), f32),
-            vmem((2, every, 2 * every), f32), vmem((2, groups) + tile, f32), vmem((2, side) + tile, f32),
-            vmem((2, side) + tile, f32), vmem((2, groups) + tile, f32), vmem((2, 3) + tile, f32),
+            vmem((every, 2 * every), f32), vmem((groups,) + tile, f32), vmem((side,) + tile, f32),
+            vmem((side,) + tile, f32), vmem((groups,) + tile, f32), vmem((3,) + tile, f32),
+            vmem((every, every), f32), vmem((groups,) + tile, f32), vmem((groups,) + tile, f32),
+            vmem((blks,) + tile, f32), vmem((groups,) + tile, f32), vmem((2,) + tile, f32),
             dma((comps + 2,)), dma((2,)), dma((2,)),
             dma((2, comps)), dma((2, comps)), dma((comps, 3)), dma((comps,)),
             dma((comps,)), dma((comps,)), dma((comps,)), dma((comps,)),
-            dma((comps,)), dma((comps,)), dma((2, comps)), dma((comps,)), dma((comps,)), dma((2, 4)), dma((2, 4)),
+            dma((comps,)), dma((comps,)), dma((2, comps)), dma((comps,)), dma((comps,)), dma((4,)), dma((4,)), dma((3,)), dma((3,)),
         ],
         compiler_params=pltpu.CompilerParams(
             collective_id=0, has_side_effects=True, vmem_limit_bytes=48 * 1024 * 1024),

time: 75.4 us -> 77.6 us (1.029)
  Pallas kernels: 73.2 us -> 75.4 us
    pallas_call x1, Pallas kernels: 73.2 us -> 75.4 us  [shards(): pl.pallas_call(functools.partial(kernel, blks, groups), out_shape=(jax.Sh...]
where the time goes in v6:
time: 77.6 us; the launch traced here: 77.5 us
  Pallas kernels  75.4 us (97%)
  local copies, waits for them, and re-layouts  1.5 us (2%)
    pallas_call x1, Pallas kernels, shards(): pl.pallas_call(functools.partial(kernel, blks, groups), out_shape=(jax.Sh...  75.4 us

profile of v6, /device:TPU:1, one launch (start us, length us, event | category | flops | bytes accessed | tf_op | source)
XLA Modules:
  0.0 77.5 jit_solution(14391841096613585613)
XLA Ops:
  0.6 75.4 %shard_map.50 = (f32[8,3,4,16,128]{4,3,2,1,0:T(8,128)S(1)}, f32[64,64]{1,0:T(8,128)S(1)}) custom-call(f32[8,3,4,16,128]{4,3,2,1,0:T(8,128)} %x_ref.1, s32[4,16,128]{2,1,0:T(8,128)} %mat_ref.1, f32[8]{0:T(128)} %tab_hbm.1), custom_call_target="tpu_custom_call" | custom-call | tf_op jit(solution)/shard_map/pallas_call | solution.py:610
  76.0 0.9 %copy.7 = f32[8,3,4,16,128]{4,3,2,1,0:T(8,128)} copy(f32[8,3,4,16,128]{4,3,2,1,0:T(8,128)S(1)} %get-tuple-element.4) | data formatting | bytes 1572864
  76.9 0.6 copy.8

commit v7 on v5

--- a/solution.py
+++ b/solution.py
@@ -245,7 +245,30 @@
             other[plane] = new
         over(3 * planes - 2 * first, body, 3 * planes - 2 * first)
 
-    def finals(comp):
+    def my_modes():
+        return pl.ds(pl.multiple_of(me * modes, modes), modes)
+
+    def spread(source, target, send, recv, comp):
+        for step in range(1, groups):
+            peer = mode_peer(step)
+            remote(source.at[comp, tile_of(peer)], target.at[comp, :, my_modes()],
+                   send.at[comp], recv.at[comp], blk, peer).start()
+
+    def spread_wait(target, send, recv, comp):
+        most = target.at[comp, :, pl.ds(0, (groups - 1) * modes)]
+        arrived(most, recv.at[comp])
+        arrived(most, send.at[comp])
+
+    def put(target, comp, plane, value):
+        for half in range(halves):
+            target[comp, plane * halves + half] = value[8 * half:8 * half + 8]
+
+    def final_filter(comp):
+        def body(plane):
+            put(filt_out, comp, plane, field[comp, planes + plane] * close[1, plane])
+        over(planes, body, planes)
+
+    def final_image(comp):
         first, last = field[comp, planes, :9], field[comp, 2 * planes - 1, 8:]
         edge_out[comp, 1, :8] = box_z(first[:8] + (first[1:] + jnp.concatenate([none, first[:7]], axis=0)))
         edge_out[comp, 0] = box_z(jnp.concatenate([none, last], axis=0) + (
@@ -268,26 +291,9 @@
         def body(plane):
             at = planes + plane
             w = field[comp, at]
-            filt = w * close[1, plane]
-            image = close[2, plane] * w - close[0, plane] * box(field[comp, at - 1] + w + field[comp, at + 1])
-            for half in range(halves):
-                filt_out[comp, plane * halves + half] = filt[8 * half:8 * half + 8]
-                image_out[comp, plane * halves + half] = image[8 * half:8 * half + 8]
+            put(image_out, comp, plane,
+                close[2, plane] * w - close[0, plane] * box(field[comp, at - 1] + w + field[comp, at + 1]))
         over(planes, body, 4)
-
-    def my_modes():
-        return pl.ds(pl.multiple_of(me * modes, modes), modes)
-
-    def spread(source, target, send, recv, comp):
-        for step in range(1, groups):
-            peer = mode_peer(step)
-            remote(source.at[comp, tile_of(peer)], target.at[comp, :, my_modes()],
-                   send.at[comp], recv.at[comp], blk, peer).start()
-
-    def spread_wait(target, send, recv, comp):
-        most = target.at[comp, :, pl.ds(0, (groups - 1) * modes)]
-        arrived(most, recv.at[comp])
-        arrived(most, send.at[comp])
 
     def filter_one(comp):
         @pl.when(jnp.logical_not(no_left))
@@ -302,17 +308,18 @@
 
         for step in range(DEGREE):
             advance(step, comp)
-        finals(comp)
+        final_filter(comp)
         spread(filt_out, filt_in, filt_send, filt_recv, comp)
 
-        @pl.when(comp + 1 < comps)
-        def _():
-            spread(image_out, image_in, image_send, image_recv, comp)
+        @pl.when(comp > 0)
+        def _():
+            spread(image_out, image_in, image_send, image_recv, comp - 1)
 
         @pl.when(comp + 2 < comps)
         def _():
             start_near(comp + 2)
 
+        final_image(comp)
         filt_in[comp, :, my_modes()] = filt_out[comp, my_tile]
         image_in[comp, :, my_modes()] = image_out[comp, my_tile]
 

time: 75.4 us -> 76.2 us (1.011)
  Pallas kernels: 73.2 us -> 74 us
    pallas_call x1, Pallas kernels: 73.2 us -> 74 us  [shards(): pl.pallas_call(functools.partial(kernel, blks, groups), out_shape=(jax.Sh...]
where the time goes in v7:
time: 76.2 us; the launch traced here: 76.1 us
  Pallas kernels  74 us (97%)
  local copies, waits for them, and re-layouts  1.5 us (2%)
    pallas_call x1, Pallas kernels, shards(): pl.pallas_call(functools.partial(kernel, blks, groups), out_shape=(jax.Sh...  74 us

profile of v7, /device:TPU:1, one launch (start us, length us, event | category | flops | bytes accessed | tf_op | source)
XLA Modules:
  0.0 76.1 jit_solution(12901490693429358300)
XLA Ops:
  0.6 74.0 %shard_map.50 = (f32[8,3,4,16,128]{4,3,2,1,0:T(8,128)S(1)}, f32[64,64]{1,0:T(8,128)S(1)}) custom-call(f32[8,3,4,16,128]{4,3,2,1,0:T(8,128)} %x_ref.1, s32[4,16,128]{2,1,0:T(8,128)} %mat_ref.1, f32[8]{0:T(128)} %tab_hbm.1), custom_call_target="tpu_custom_call" | custom-call | tf_op jit(solution)/shard_map/pallas_call | solution.py:567
  74.6 0.9 %copy.7 = f32[8,3,4,16,128]{4,3,2,1,0:T(8,128)} copy(f32[8,3,4,16,128]{4,3,2,1,0:T(8,128)S(1)} %get-tuple-element.4) | data formatting | bytes 1572864
  75.5 0.6 copy.8

commit v8 on v7

--- a/solution.py
+++ b/solution.py
@@ -311,7 +311,7 @@
         final_filter(comp)
         spread(filt_out, filt_in, filt_send, filt_recv, comp)
 
-        @pl.when(comp > 0)
+        @pl.when(comp + 1 == comps)
         def _():
             spread(image_out, image_in, image_send, image_recv, comp - 1)
 
@@ -320,6 +320,11 @@
             start_near(comp + 2)
 
         final_image(comp)
+
+        @pl.when(comp + 2 < comps)
+        def _():
+            spread(image_out, image_in, image_send, image_recv, comp)
+
         filt_in[comp, :, my_modes()] = filt_out[comp, my_tile]
         image_in[comp, :, my_modes()] = image_out[comp, my_tile]
 

time: 76.2 us -> 72.4 us (0.950)
  Pallas kernels: 74 us -> 70.1 us
    pallas_call x1, Pallas kernels: 74 us -> 70.1 us  [shards(): pl.pallas_call(functools.partial(kernel, blks, groups), out_shape=(jax.Sh...]
where the time goes in v8:
time: 72.4 us; the launch traced here: 72.3 us
  Pallas kernels  70.1 us (97%)
  local copies, waits for them, and re-layouts  1.5 us (2%)
    pallas_call x1, Pallas kernels, shards(): pl.pallas_call(functools.partial(kernel, blks, groups), out_shape=(jax.Sh...  70.1 us
    unnamed x2, local copies, waits for them, and re-layouts  1.5 us

profile of v8, /device:TPU:1, one launch (start us, length us, event | category | flops | bytes accessed | tf_op | source)
XLA Modules:
  0.0 72.3 jit_solution(16266276913630088876)
XLA Ops:
  0.6 70.1 %shard_map.50 = (f32[8,3,4,16,128]{4,3,2,1,0:T(8,128)S(1)}, f32[64,64]{1,0:T(8,128)S(1)}) custom-call(f32[8,3,4,16,128]{4,3,2,1,0:T(8,128)} %x_ref.1, s32[4,16,128]{2,1,0:T(8,128)} %mat_ref.1, f32[8]{0:T(128)} %tab_hbm.1), custom_call_target="tpu_custom_call" | custom-call | tf_op jit(solution)/shard_map/pallas_call | solution.py:572
  70.8 0.9 %copy.7 = f32[8,3,4,16,128]{4,3,2,1,0:T(8,128)} copy(f32[8,3,4,16,128]{4,3,2,1,0:T(8,128)S(1)} %get-tuple-element.4) | data formatting | bytes 1572864
  71.7 0.6 copy.8

commit v9 on v8

--- a/solution.py
+++ b/solution.py
@@ -228,6 +228,10 @@
     def box(u):
         return box_z(u + (jnp.concatenate([none, u[:-1]], axis=0) + jnp.concatenate([u[1:], none], axis=0)))
 
+    def put(target, comp, plane, value):
+        for half in range(halves):
+            target[comp, plane * halves + half] = value[8 * half:8 * half + 8]
+
     def advance(step, comp):
         even = field.at[comp]
         now, other = (even, odd) if step % 2 == 0 else (odd, even)
@@ -243,6 +247,8 @@
             else:
                 new = new - other[plane]
             other[plane] = new
+            if step == DEGREE - 1:
+                put(filt_out, comp, plane - planes, new * close[1, plane - planes])
         over(3 * planes - 2 * first, body, 3 * planes - 2 * first)
 
     def my_modes():
@@ -258,15 +264,6 @@
         most = target.at[comp, :, pl.ds(0, (groups - 1) * modes)]
         arrived(most, recv.at[comp])
         arrived(most, send.at[comp])
-
-    def put(target, comp, plane, value):
-        for half in range(halves):
-            target[comp, plane * halves + half] = value[8 * half:8 * half + 8]
-
-    def final_filter(comp):
-        def body(plane):
-            put(filt_out, comp, plane, field[comp, planes + plane] * close[1, plane])
-        over(planes, body, planes)
 
     def final_image(comp):
         first, last = field[comp, planes, :9], field[comp, 2 * planes - 1, 8:]
@@ -308,7 +305,6 @@
 
         for step in range(DEGREE):
             advance(step, comp)
-        final_filter(comp)
         spread(filt_out, filt_in, filt_send, filt_recv, comp)
 
         @pl.when(comp + 1 == comps)

time: 72.4 us -> 72.4 us (level)
  no operation moved by 1% of the time
where the time goes in v9:
time: 72.4 us; the launch traced here: 72.3 us
  Pallas kernels  70.1 us (97%)
  local copies, waits for them, and re-layouts  1.5 us (2%)
    pallas_call x1, Pallas kernels, shards(): pl.pallas_call(functools.partial(kernel, blks, groups), out_shape=(jax.Sh...  70.1 us
    unnamed x2, local copies, waits for them, and re-layouts  1.5 us

profile of v9, /device:TPU:1, one launch (start us, length us, event | category | flops | bytes accessed | tf_op | source)
XLA Modules:
  0.0 72.3 jit_solution(16266276913630088876)
XLA Ops:
  0.6 70.1 %shard_map.50 = (f32[8,3,4,16,128]{4,3,2,1,0:T(8,128)S(1)}, f32[64,64]{1,0:T(8,128)S(1)}) custom-call(f32[8,3,4,16,128]{4,3,2,1,0:T(8,128)} %x_ref.1, s32[4,16,128]{2,1,0:T(8,128)} %mat_ref.1, f32[8]{0:T(128)} %tab_hbm.1), custom_call_target="tpu_custom_call" | custom-call | tf_op jit(solution)/shard_map/pallas_call | solution.py:568
  70.8 0.9 %copy.7 = f32[8,3,4,16,128]{4,3,2,1,0:T(8,128)} copy(f32[8,3,4,16,128]{4,3,2,1,0:T(8,128)S(1)} %get-tuple-element.4) | data formatting | bytes 1572864
  71.7 0.6 copy.8
